TPU v7x, 256 devices: a whole 4x4x8 slice. The times are simulated.
256 devices in a mesh: grp: 4 (over x), tile: 64 (over z, y, core).
Axes of the slice: x: 4, y: 4, z: 8, core: 2. Of those that a mesh axis runs over, the one named last changes fastest.
Arguments:
- obs_anom: bfloat16 [8192, 64, 256], P(('grp', 'tile')), may hold values from -6 to 6
- innov: bfloat16 [8192, 64, 256], P(('grp', 'tile')), may hold values from -6 to 6
- obs_rinv: float32 [8192, 64], P(('grp', 'tile')), may hold values from 0.5 to 5
- obs_pos: int32 [8192, 64], P(('grp', 'tile')), may hold values from 0 to 32767
- obs_count: int32 [8192], P(('grp', 'tile')), may hold values from 1 to 64
- obs_region: int32 [8192, 1], P(('grp', 'tile')), may hold values from 0 to 63; in each aligned block of 32 rows (0 to 31, 32 to 63, ...) at most 2 rows name the same one
- obs_partner: int32 [8192, 6], P(('grp', 'tile')), may hold values from 0 to 7, all different within a row
- state_anom: bfloat16 [4, 128, 4096, 256], P('grp', 'tile'), may hold values from -6 to 6
- coeff: float32 [4, 128, 256, 256], P('grp', 'tile'), may hold values from -0.375 to 0.375
Outputs:
- updated: bfloat16 [4, 128, 4096, 256], P('grp', 'tile')
- new_coeff: float32 [4, 128, 256, 256], P('grp', 'tile')
Inputs may be any that keep to these rules, and one draw needn't show every extreme that they name: `obs_region`: among the 32 observation blocks of one device (aligned blocks of rows), no region is named more than 2 times; some region is named exactly 2 times. `obs_partner`: the 6 partners of one observation block are different.
All inputs are finite; a program needn't handle non-finite values.
Results may differ from a plain program's by a relative error of at most 0.02.
Values may be sent and summed in bfloat16 or wider, within the bound.
A program may use at most 192 MiB of HBM per device.

v0:
```python
import jax
import jax.numpy as jnp
from jax import lax
from jax.sharding import PartitionSpec as P

relaxation = 0.5


def taper_weights(positions, partners, counts, inverse_var, width, ensemble_members):
    center = (partners.astype(jnp.float32) + 0.5) * width
    offset = (positions.astype(jnp.float32)[..., None, :] - center[..., :, None]) / (2.0 * width)
    index = jnp.arange(positions.shape[-1], dtype=jnp.int32)
    live = index < counts[..., None]
    weight = jnp.exp(-offset * offset) * inverse_var[..., None, :] / (ensemble_members - 1.0)
    return jnp.where(live[..., None, :], weight, 0.0)


def on_device(
    obs_anom, innov, obs_rinv, obs_pos, obs_count, obs_region, obs_partner, state_anom, coeff
):
    tile_count = lax.axis_size("tile")
    nblock, observation_count, ensemble_members = obs_anom.shape
    width = state_anom.shape[2]
    partition_count = obs_partner.shape[1]
    nlocal = lax.axis_size("grp") * state_anom.shape[1]
    per_neighbour = max(2, (2 * nblock + tile_count - 1) // tile_count)
    slot_count = tile_count * per_neighbour
    slot_grouping = 8
    region = obs_region[:, 0]
    order = jnp.arange(nblock, dtype=jnp.int32)
    before = (region[None, :] == region[:, None]) & (order[None, :] < order[:, None])
    destination = region * per_neighbour + jnp.sum(before.astype(jnp.int32), axis=1)
    assignment_rule = destination[None, :] == jnp.arange(slot_count, dtype=jnp.int32)[:, None]
    place_half = assignment_rule.astype(jnp.bfloat16)
    place_int = assignment_rule.astype(jnp.int32)
    labels = jnp.concatenate([obs_count[:, None], obs_partner], axis=1)
    sent_labels = jnp.dot(place_int, labels).reshape(tile_count, per_neighbour, partition_count + 1)
    anomalies = state_anom[0]
    base_coef = ((1.0 - relaxation) * coeff[0]).astype(jnp.bfloat16)
    base_part = jnp.einsum("sbm,smn->sbn", anomalies, base_coef, preferred_element_type=jnp.float32)
    stacked = jnp.concatenate([obs_anom, innov], axis=2).reshape(nblock, -1)
    packed = jnp.dot(place_half, stacked, preferred_element_type=jnp.bfloat16)
    packed = packed.reshape(tile_count, per_neighbour, observation_count, 2 * ensemble_members)
    sent_pos = jnp.dot(place_int, obs_pos).reshape(tile_count, per_neighbour, observation_count)
    sent_var = jnp.dot(
        assignment_rule.astype(jnp.float32), obs_rinv, precision=lax.Precision.HIGHEST
    )
    sent_var = sent_var.reshape(tile_count, per_neighbour, observation_count)
    received_panels, received_labels, received_positions, received_variances = (
        lax.all_to_all(packed, "tile", split_axis=0, concat_axis=0, tiled=True),
        lax.all_to_all(sent_labels, "tile", split_axis=0, concat_axis=0, tiled=True),
        lax.all_to_all(sent_pos, "tile", split_axis=0, concat_axis=0, tiled=True),
        lax.all_to_all(
            sent_var.astype(jnp.bfloat16), "tile", split_axis=0, concat_axis=0, tiled=True
        ).astype(sent_var.dtype),
    )
    received_panels = received_panels.reshape(slot_count, observation_count, 2 * ensemble_members)
    flattened_labels = received_labels.reshape(slot_count, partition_count + 1)
    recv_anom = received_panels[:, :, :ensemble_members]
    recv_innov = received_panels[:, :, ensemble_members:]
    flattened_positions = received_positions.reshape(slot_count, observation_count)
    flattened_variances = received_variances.reshape(slot_count, observation_count)

    def scaled_slice(start):
        innov_part = lax.dynamic_slice_in_dim(recv_innov, start, slot_grouping, 0)
        pos_part = lax.dynamic_slice_in_dim(flattened_positions, start, slot_grouping, 0)
        var_part = lax.dynamic_slice_in_dim(flattened_variances, start, slot_grouping, 0)
        label_part = lax.dynamic_slice_in_dim(flattened_labels, start, slot_grouping, 0)
        weights = taper_weights(
            pos_part, label_part[:, 1:], label_part[:, 0], var_part, width, ensemble_members
        )
        return (weights[..., None] * innov_part[:, None].astype(jnp.float32)).astype(jnp.bfloat16)

    partners = flattened_labels[:, 1:]
    block_index = jnp.arange(nlocal, dtype=jnp.int32)

    def accumulate_group(step, total):
        start = step * slot_grouping
        anom_part = lax.dynamic_slice_in_dim(recv_anom, start, slot_grouping, 0)
        partner_part = lax.dynamic_slice_in_dim(partners, start, slot_grouping, 0)
        scaled_part = scaled_slice(start)
        picked = (partner_part[..., None] == block_index).astype(jnp.bfloat16)
        by_block = jnp.einsum(
            "qkb,qkin->qbin", picked, scaled_part, preferred_element_type=jnp.float32
        ).astype(jnp.bfloat16)
        return total + jnp.einsum(
            "qim,qbin->bmn", anom_part, by_block, preferred_element_type=jnp.float32
        )

    initial_total = jnp.zeros((nlocal, ensemble_members, ensemble_members), jnp.float32)
    running_totals = lax.fori_loop(0, slot_count // slot_grouping, accumulate_group, initial_total)
    mine = lax.psum_scatter(
        running_totals.astype(jnp.bfloat16), "grp", scatter_dimension=0, tiled=True
    ).astype(jnp.float32)
    new_coeff = (1.0 - relaxation) * coeff[0] + relaxation * mine
    gain_coef = (relaxation * mine).astype(jnp.bfloat16)
    gain_part = jnp.einsum("sbm,smn->sbn", anomalies, gain_coef, preferred_element_type=jnp.float32)
    updated = (anomalies.astype(jnp.float32) + base_part + gain_part).astype(jnp.bfloat16)
    return (updated[None], new_coeff[None])


def solution(mesh):
    return jax.shard_map(
        on_device,
        mesh=mesh,
        in_specs=(
            P(("grp", "tile"), None, None),
            P(("grp", "tile"), None, None),
            P(("grp", "tile"), None),
            P(("grp", "tile"), None),
            P(("grp", "tile")),
            P(("grp", "tile"), None),
            P(("grp", "tile"), None),
            P("grp", "tile", None, None),
            P("grp", "tile", None, None),
        ),
        out_specs=(P("grp", "tile", None, None), P("grp", "tile", None, None)),
        check_vma=False,
    )
```

profile of v0, /device:TPU:8, one launch (start us, length us, event | category | flops | bytes accessed | tf_op | source)
XLA Modules:
  0.0 432.3 jit_solution(16011732630365613588)
XLA Ops:
  10.2 12.1 %all-to-all-start = ((s32[64,2,7]{2,1,0:T(2,128)}), s32[64,2,7]{2,1,0:T(2,128)S(1)}, u32[]{:S(2)}, u32[]{:S(2)}) async-start(s32[64,2,7]{2,1,0:T(2,128)} %bitcast.6), calls=%async_computation | async-start | bytes 131072 | tf_op jit(solution)/shard_map/all_to_all | solution.py:51
  25.9 5.3 %all-to-all-done = s32[64,2,7]{2,1,0:T(2,128)S(1)} async-done(((s32[64,2,7]{2,1,0:T(2,128)}), s32[64,2,7]{2,1,0:T(2,128)S(1)}, u32[]{:S(2)}, u32[]{:S(2)}) %all-to-all-start) | async-done | bytes 3616 | tf_op jit(solution)/shard_map/all_to_all | solution.py:51
  31.3 5.6 %all-to-all-start.2 = ((bf16[64,2,64]{2,1,0:T(2,128)(2,1)}), bf16[64,2,64]{2,1,0:T(2,128)(2,1)S(1)}, u32[]{:S(2)}, u32[]{:S(2)}) async-start(bf16[64,2,64]{2,1,0:T(2,128)(2,1)} %bitcast.10), calls=%async_computation.2 | async-start | bytes 65536 | tf_op jit(solution)/shard_map/all_to_all | solution.py:53
  37.6 7.9 %all-to-all-done.2 = bf16[64,2,64]{2,1,0:T(2,128)(2,1)S(1)} async-done(((bf16[64,2,64]{2,1,0:T(2,128)(2,1)}), bf16[64,2,64]{2,1,0:T(2,128)(2,1)S(1)}, u32[]{:S(2)}, u32[]{:S(2)}) %all-to-all-start.2) | async-done | bytes 16416 | tf_op jit(solution)/shard_map/all_to_all | solution.py:53
  45.5 5.5 %all-to-all-start.1 = ((s32[64,1,128]{2,1,0:T(1,128)}), s32[64,1,128]{2,1,0:T(1,128)S(1)}, u32[]{:S(2)}, u32[]{:S(2)}) async-start(s32[64,1,128]{2,1,0:T(1,128)} %reshape.111), calls=%async_computation.1 | async-start | bytes 65536 | tf_op jit(solution)/shard_map/all_to_all | solution.py:52
  51.0 5.7 %fusion.25 = bf16[64,2,64,512]{3,0,2,1:T(8,128)(2,1)} fusion(s32[64,2]{0,1:T(2,128)S(1)} %multiply_add_fusion, s32[32]{0:T(128)S(1)} %multiply_add_fusion.1, bf16[4,8,64,512]{3,2,1,0:T(8,128)(2,1)S(1)} %bitcast.87), kind=kOutput, calls=%fused_computation.35 | convolution fusion | flops 268439552 | bytes 10486400 | tf_op jit(solution)/shard_map/dot_general | solution.py:42
  56.7 11.4 %copy.62 = bf16[64,2,64,512]{3,2,1,0:T(8,128)(2,1)} copy(bf16[64,2,64,512]{3,0,2,1:T(8,128)(2,1)} %fusion.25) | data formatting | bytes 16777216 | tf_op jit(solution)/shard_map/dot_general | solution.py:42
  68.0 10.6 %all-to-all-start.3 = ((bf16[64,2,64,512]{3,2,1,0:T(8,128)(2,1)}), bf16[64,2,64,512]{3,2,1,0:T(8,128)(2,1)}, u32[]{:S(2)}, u32[]{:S(2)}) async-start(bf16[64,2,64,512]{3,2,1,0:T(8,128)(2,1)} %copy.62), calls=%async_computation.3 | async-start | bytes 16777216 | tf_op jit(solution)/shard_map/all_to_all | solution.py:50
  80.1 183.5 %all-to-all-done.3 = bf16[64,2,64,512]{3,2,1,0:T(8,128)(2,1)} async-done(((bf16[64,2,64,512]{3,2,1,0:T(8,128)(2,1)}), bf16[64,2,64,512]{3,2,1,0:T(8,128)(2,1)}, u32[]{:S(2)}, u32[]{:S(2)}) %all-to-all-start.3) | async-done | bytes 8388640 | tf_op jit(solution)/shard_map/all_to_all | solution.py:50
  263.6 6.1 %fusion.48 = (bf16[128,64,256]{2,1,0:T(8,128)(2,1)}, bf16[128,64,256]{2,1,0:T(8,128)(2,1)}) fusion(bf16[128,64,512]{2,1,0:T(8,128)(2,1)} %bitcast.16), kind=kLoop, calls=%fused_computation.67 | loop fusion | bytes 16777216 | tf_op jit(solution)/shard_map/slice | solution.py:59
  269.8 112.9 %while.14 = (s32[]{:T(128)}, f32[8,256,256]{1,2,0:T(8,128)S(1)}, s32[128,6]{1,0:T(8,128)S(1)}, s32[128,7]{1,0:T(8,128)S(1)}, s32[128,64]{1,0:T(8,128)S(1)}, /*in...) while((s32[]{:T(128)}, f32[8,256,256]{1,2,0:T(8,128)S(1)}, ...), condition=%wide.region_2.3_spmd.clone, body=%wide.region_1.2_spmd.clone.sunk | while | flops 553277952 | bytes 10002405 | solution.py:91
  273.6 3.2 bitcast_add_fusion.5
  280.7 3.2 bitcast_add_fusion.5
  287.7 3.2 bitcast_add_fusion.5
  294.8 3.2 bitcast_add_fusion.5
  301.8 3.2 bitcast_add_fusion.5
  308.9 3.2 bitcast_add_fusion.5
  315.9 3.2 bitcast_add_fusion.5
  323.0 3.2 bitcast_add_fusion.5
  384.1 6.4 %copy.55 = bf16[1,2,4096,256]{2,3,1,0:T(8,128)(2,1)} copy(bf16[1,2,4096,256]{3,2,1,0:T(8,128)(2,1)} %param.18) | data formatting | bytes 8388608 | tf_op args[7]
  390.5 6.7 %fusion.22 = f32[2,256,4096]{2,1,0:T(8,128)} fusion(bf16[1,2,4096,256]{3,2,1,0:T(8,128)(2,1)} %param.18, f32[1,2,256,256]{3,2,1,0:T(8,128)S(1)} %copy-done.2), kind=kOutput, calls=%fused_computation.31 | convolution fusion | flops 1074003968 | bytes 13107200 | tf_op jit(solution)/shard_map/sbm,smn->sbn/dot_general | solution.py:40
  397.3 11.3 %reduce-scatter.2.cloned.1.call-done = bf16[2,256,256]{2,1,0:T(8,128)(2,1)} async-done(((bf16[8,256,256]{2,1,0:T(8,128)(2,1)}), bf16[2,256,256]{2,1,0:T(8,128)(2,1)}) %reduce-scatter.2.cloned.1.call-update) | async-done | bytes 262160 | tf_op jit(solution)/shard_map/reduce_scatter | solution.py:92
  408.6 9.6 %fusion.21 = bf16[1,2,4096,256]{2,3,1,0:T(8,128)(2,1)} fusion(f32[2,256,4096]{2,1,0:T(8,128)} %fusion.22, bf16[1,2,4096,256]{3,2,1,0:T(8,128)(2,1)} %param.18, bf16[1,2,4096,256]{2,3,1,0:T(8,128)(2,1)} %copy.55, bf16[2,256,256]{2,1,0:T(8,128)(2,1)} %reduce-scatter.2.cloned.1.call-done), kind=kOutput, calls=%fused_computation.30 | convolution fusion | flops 1082523648 | bytes 21233664 | tf_op jit(solution)/shard_map/sbm,smn->sbn/dot_general | solution.py:97
  418.2 6.4 %copy.67 = bf16[1,2,4096,256]{3,2,1,0:T(8,128)(2,1)} copy(bf16[1,2,4096,256]{2,3,1,0:T(8,128)(2,1)} %fusion.21) | data formatting | bytes 8388608
  (244 shorter events, 97.4 us)
Async XLA Ops:
  7.2 15.2 %copy-start = (s32[32,64]{1,0:T(8,128)S(1)}, s32[32,64]{1,0:T(8,128)}, u32[]{:S(2)}) copy-start(s32[32,64]{1,0:T(8,128)} %param.14) | copy-start | bytes 24580
  10.2 21.0 %all-to-all-start = ((s32[64,2,7]{2,1,0:T(2,128)}), s32[64,2,7]{2,1,0:T(2,128)S(1)}, u32[]{:S(2)}, u32[]{:S(2)}) async-start(s32[64,2,7]{2,1,0:T(2,128)} %bitcast.6), calls=%async_computation | async-start | bytes 131072 | tf_op jit(solution)/shard_map/all_to_all | solution.py:51
  31.3 14.2 %all-to-all-start.2 = ((bf16[64,2,64]{2,1,0:T(2,128)(2,1)}), bf16[64,2,64]{2,1,0:T(2,128)(2,1)S(1)}, u32[]{:S(2)}, u32[]{:S(2)}) async-start(bf16[64,2,64]{2,1,0:T(2,128)(2,1)} %bitcast.10), calls=%async_computation.2 | async-start | bytes 65536 | tf_op jit(solution)/shard_map/all_to_all | solution.py:53
  45.5 22.5 %all-to-all-start.1 = ((s32[64,1,128]{2,1,0:T(1,128)}), s32[64,1,128]{2,1,0:T(1,128)S(1)}, u32[]{:S(2)}, u32[]{:S(2)}) async-start(s32[64,1,128]{2,1,0:T(1,128)} %reshape.111), calls=%async_computation.1 | async-start | bytes 65536 | tf_op jit(solution)/shard_map/all_to_all | solution.py:52
  68.0 195.6 %all-to-all-start.3 = ((bf16[64,2,64,512]{3,2,1,0:T(8,128)(2,1)}), bf16[64,2,64,512]{3,2,1,0:T(8,128)(2,1)}, u32[]{:S(2)}, u32[]{:S(2)}) async-start(bf16[64,2,64,512]{3,2,1,0:T(8,128)(2,1)} %copy.62), calls=%async_computation.3 | async-start | bytes 16777216 | tf_op jit(solution)/shard_map/all_to_all | solution.py:50
  78.6 329.9 %reduce-scatter.2.cloned.1.call-start = ((), (), s32[]{:S(2)}) async-start(), calls=%async_computation.5 | async-start | bytes 1310720 | tf_op jit(solution)/shard_map/reduce_scatter | solution.py:92
  384.1 6.4 %copy-start.2 = (f32[1,2,256,256]{3,2,1,0:T(8,128)S(1)}, f32[1,2,256,256]{3,2,1,0:T(8,128)}, u32[]{:S(2)}) copy-start(f32[1,2,256,256]{3,2,1,0:T(8,128)} %param.19) | copy-start | bytes 1572868
  408.5 16.9 %copy-start.1 = (s32[32,64]{1,0:T(8,128)S(1)}, s32[32,64]{1,0:T(8,128)}, u32[]{:S(2)}) copy-start(s32[32,64]{1,0:T(8,128)} %param.14) | copy-start | bytes 24580
  418.2 6.4 %copy-start.3 = (bf16[2,256,256]{2,1,0:T(8,128)(2,1)S(1)}, bf16[2,256,256]{2,1,0:T(8,128)(2,1)}, u32[]{:S(2)}) copy-start(bf16[2,256,256]{2,1,0:T(8,128)(2,1)} %reduce-scatter.2.cloned.1.call-done) | copy-start | bytes 786436
Sparse Core Ops, SparseCore 0:
  384.3 24.2 reduce-scatter.1
where the time goes:
time: 434 us; the launch traced here: 432 us
  waiting for transfers between devices  208 us (48%)
  matrix products  110 us (25%)
  local copies, waits for them, and re-layouts  39.3 us (9%)
  starting transfers between devices  33.8 us (8%)
  other arithmetic  26.5 us (6%)
  between operations  14.2 us (3%)
    all_to_all x1, waiting for transfers between devices, on_device(): lax.all_to_all(packed, 'tile', split_axis=0, concat_axis=0, tiled=True)  184 us
    dot_general x16, matrix products, accumulate_group(): jnp.einsum('qim,qbin->bmn', anom_part, by_block, preferred_element_type=j...  51.4 us
    dot_general x16, matrix products, accumulate_group(): jnp.einsum('qkb,qkin->qbin', picked, scaled_part, preferred_element_type=...  33.5 us
    convert_element_type x16, other arithmetic, scaled_slice(): innov_part[:, None].astype(jnp.float32)  15.9 us
    unnamed x12, local copies, waits for them, and re-layouts  13.6 us
    all_to_all x1, starting transfers between devices, on_device(): lax.all_to_all(sent_labels, 'tile', split_axis=0, concat_axis=0, tiled=True)  12.1 us
    dot_general x1, local copies, waits for them, and re-layouts, on_device(): packed = jnp.dot(place_half, stacked, preferred_element_type=jnp.bfloat16)  11.4 us
    reduce_scatter x1, waiting for transfers between devices, on_device(): lax.psum_scatter(running_totals.astype(jnp.bfloat16), 'grp', scatter_dime...  11.3 us
  transfers between devices with their start and end apart: 5, of which 4 were waited for; matrix products, arithmetic and copies ran while one was open for 8% of the time, Pallas kernels for 0%

commit v1 on v0

v1 whole, which is shorter than its diff:
```python
import jax
import jax.numpy as jnp
from jax import lax
from jax.experimental import pallas as pl
from jax.experimental.pallas import tpu as pltpu
from jax.sharding import PartitionSpec as P

relaxation = 0.5
bf16, f32, i32 = jnp.bfloat16, jnp.float32, jnp.int32
MESH = pl.DeviceIdType.MESH
MIB = 1024 * 1024

ROWS = 16
CAPS = (64, 54, 42, 30)
STAY = 40
RING = sum(CAPS)
SEND = 2 * CAPS[0] + STAY
HOPS = len(CAPS)
NZ, NY, NX, NR = 8, 4, 4, 64
LISTS = 2 * HOPS


def hop_base(way, hop):
    return way * RING + sum(CAPS[:hop])


def taper_weights(positions, partners, counts, inverse_var, width, ensemble_members):
    center = (partners.astype(jnp.float32) + 0.5) * width
    offset = (positions.astype(jnp.float32)[..., None, :] - center[..., :, None]) / (2.0 * width)
    index = jnp.arange(positions.shape[-1], dtype=jnp.int32)
    live = index < counts[..., None]
    weight = jnp.exp(-offset * offset) * inverse_var[..., None, :] / (ensemble_members - 1.0)
    return jnp.where(live[..., None, :], weight, 0.0)


def pack_kernel(region, count, partner, pos, rinv, anom, innov, send, send_w, head, wall, size, fill, first, seat_a, seat_b):
    nblock, members = anom.shape[0], anom.shape[2]
    width = 4096.0
    z = lax.axis_index("tile") // 8

    grain = lax.broadcasted_iota(i32, (128, 128), 0)
    lane = lax.broadcasted_iota(i32, (128, 128), 1)
    repeat = (lax.broadcasted_iota(i32, (128, nblock), 0) // 4 == lax.broadcasted_iota(i32, (128, nblock), 1)).astype(f32)
    column = lax.broadcasted_iota(i32, (128, 64), 1)
    quarter = (column // 16 == lax.broadcasted_iota(i32, (128, 64), 0) % 4).astype(f32)
    fold = (lax.broadcasted_iota(i32, (64, 128), 0) % 16 == lax.broadcasted_iota(i32, (64, 128), 1) % 16).astype(f32)

    def exact(a, b):
        return jnp.dot(a, b, precision=lax.Precision.HIGHEST, preferred_element_type=f32)

    def spread(values):
        return exact(exact(repeat, values) * quarter, fold)

    paired = jnp.zeros((nblock, 128), f32)
    block_of_lane = lax.broadcasted_iota(i32, (nblock, 128), 1) // 16
    for k in range(partner.shape[1]):
        paired = jnp.where(partner[:, k : k + 1] == block_of_lane, 1.0, paired)
    center = ((lane // 16).astype(f32) + 0.5) * width
    offset = (spread(pos[...].astype(f32)) - center) / (2.0 * width)
    wall[...] = jnp.exp(-offset * offset) * spread(rinv[...]) / (members - 1.0) * exact(repeat, paired)

    def clear(i, c):
        size[i] = 0
        fill[i] = 0
        for row in range(2):
            head[row, i] = 0
            head[row, i + NR] = 0
        return c

    lax.fori_loop(0, NR, clear, 0)

    def measure(o, c):
        r = region[o, 0]
        size[r] = size[r] + (count[o] + 15) // 16
        return c

    lax.fori_loop(0, nblock, measure, 0)

    def plane(distance):
        return lax.rem(z + distance, NZ) * 8

    def total(distance):
        base = plane(distance)
        return sum(size[base + i] for i in range(8))

    d = [total(distance) for distance in range(NZ)]
    right, left = d[1] + d[2] + d[3], d[5] + d[6] + d[7]
    far_right = jnp.clip((d[4] + left - right + 1) // 2, 0, d[4])
    far_left = d[4] - far_right
    loads = (
        (right + far_right, d[2] + d[3] + far_right, d[3] + far_right, far_right),
        (left + far_left, d[6] + d[5] + far_left, d[5] + far_left, far_left),
    )
    over = (d[0] > STAY).astype(i32)
    for way in range(2):
        for hop in range(HOPS):
            over = over | (loads[way][hop] > CAPS[hop]).astype(i32)
    head[1, NR] = over

    def seat_far(i, used):
        used_right, used_left = used
        r = plane(4) + i
        n = size[r]
        a = jnp.minimum(n, far_right - used_right)
        b = n - a
        head[0, r] = used_right * 256 + a
        head[0, NR + r] = used_left * 256 + b
        first[r] = a
        seat_a[r] = used_right
        seat_b[r] = CAPS[0] + used_left
        return used_right + a, used_left + b

    used_right, used_left = lax.fori_loop(0, 8, seat_far, (jnp.int32(0), jnp.int32(0)))

    def seat_near(distance, base, row, shift, used):
        def seat(i, used):
            r = plane(distance) + i
            n = size[r]
            head[row, shift + r] = used * 256 + n
            first[r] = n
            seat_a[r] = base + used
            seat_b[r] = base + used
            return used + n

        return lax.fori_loop(0, 8, seat, used)

    for distance in (3, 2, 1):
        used_right = seat_near(distance, 0, 0, 0, used_right)
    for distance in (5, 6, 7):
        used_left = seat_near(distance, CAPS[0], 0, NR, used_left)
    seat_near(0, 2 * CAPS[0], 1, 0, jnp.int32(0))

    row_of_lane = lax.broadcasted_iota(i32, (1, 128), 1) % 16

    def place(o, c):
        r, live = region[o, 0], count[o]
        grains = (live + 15) // 16
        start = fill[r]
        fill[r] = start + grains
        a, b, most = seat_a[r], seat_b[r], first[r]

        def one(q, c):
            f = start + q
            slot = jnp.minimum(jnp.where(f < most, a + f, b + f - most), SEND - 1)
            rows = pl.ds(pl.multiple_of(q * ROWS, ROWS), ROWS)
            send[slot, :, 0:members] = anom[o, rows, :]
            send[slot, :, members : 2 * members] = innov[o, rows, :]
            weight = wall[pl.ds(o * 4 + q, 1), :]
            send_w[pl.ds(slot, 1), :] = jnp.where(row_of_lane < live - q * ROWS, weight, 0.0)
            return c

        return lax.fori_loop(0, grains, one, c)

    lax.fori_loop(0, nblock, place, 0)


def pack(region, count, partner, pos, rinv, anom, innov):
    members = anom.shape[2]
    vmem, smem = pl.BlockSpec(memory_space=pltpu.VMEM), pl.BlockSpec(memory_space=pltpu.SMEM)
    return pl.pallas_call(
        pack_kernel,
        out_shape=(
            jax.ShapeDtypeStruct((SEND, ROWS, 2 * members), bf16),
            jax.ShapeDtypeStruct((SEND, 128), f32),
            jax.ShapeDtypeStruct((8, 128), i32),
        ),
        in_specs=[smem, smem, vmem, vmem, vmem, vmem, vmem],
        out_specs=(vmem, vmem, smem),
        scratch_shapes=[pltpu.VMEM((128, 128), f32)] + [pltpu.SMEM((NR,), i32)] * 5,
        compiler_params=pltpu.CompilerParams(vmem_limit_bytes=32 * MIB),
    )(region, count, partner, pos, rinv, anom, innov)


def ring_kernel(send, send_w, head, zm, zs, wm, ws, hm, hs, zsend, zrecv, ssend, srecv, osend, orecv):
    tile = lax.axis_index("tile")
    z, inner = tile // 8, tile % 8
    ways = (lax.rem(z + 1, NZ) * 8 + inner, lax.rem(z + NZ - 1, NZ) * 8 + inner)
    sibling = tile + 1 - 2 * (tile % 2)

    barrier = pltpu.get_barrier_semaphore()
    for other in (*ways, sibling):
        pl.semaphore_signal(barrier, inc=1, device_id={"tile": other}, device_id_type=MESH)
    pl.semaphore_wait(barrier, 3)

    def copy(src, dst, send_sem, recv_sem, other):
        return pltpu.make_async_remote_copy(
            src_ref=src, dst_ref=dst, send_sem=send_sem, recv_sem=recv_sem, device_id={"tile": other}, device_id_type=MESH
        )

    edges = (0, *CAPS[::-1])

    def hop_copies(way, hop):
        out = []
        for k in range(HOPS - hop):
            lo, n = edges[k], edges[k + 1] - edges[k]
            if hop == 0:
                src = send.at[pl.ds(way * CAPS[0] + lo, n)]
            else:
                src = zm.at[pl.ds(hop_base(way, hop - 1) + lo, n)]
            out.append((k, src, zm.at[pl.ds(hop_base(way, hop) + lo, n)]))
        entry = way * HOPS + hop
        src_w = send_w.at[pl.ds(way * CAPS[0], CAPS[0])] if hop == 0 else wm.at[entry - 1]
        src_h = head if hop == 0 else hm.at[entry - 1]
        out.append((4, src_w, wm.at[entry]))
        out.append((5, src_h, hm.at[entry]))
        return {
            k: copy(src, dst, zsend.at[way, hop, k], zrecv.at[way, hop, k], ways[way]) for k, src, dst in out
        }

    def sibling_copies(way, hop):
        entry = way * HOPS + hop
        span = pl.ds(hop_base(way, hop), CAPS[hop])
        pairs = ((zm.at[span], zs.at[span]), (wm.at[entry], ws.at[entry]), (hm.at[entry], hs.at[entry]))
        return [copy(s, t, ssend.at[entry, i], srecv.at[entry, i], sibling) for i, (s, t) in enumerate(pairs)]

    z_copies = [[hop_copies(way, hop) for hop in range(HOPS)] for way in range(2)]
    order = [[5, 4, *range(HOPS - hop)] for hop in range(HOPS)]
    for k in order[0]:
        for way in range(2):
            z_copies[way][0][k].start()
    side = [
        copy(send.at[pl.ds(2 * CAPS[0], STAY)], zs.at[pl.ds(2 * RING, STAY)], osend.at[0], orecv.at[0], sibling),
        copy(send_w.at[pl.ds(2 * CAPS[0], STAY)], ws.at[LISTS, pl.ds(0, STAY)], osend.at[1], orecv.at[1], sibling),
        copy(head, hs.at[LISTS], osend.at[2], orecv.at[2], sibling),
    ]
    for c in side:
        c.start()
    for hop in range(HOPS):
        for k in order[hop]:
            for way in range(2):
                z_copies[way][hop][k].wait_recv()
                if hop + 1 < HOPS and k in z_copies[way][hop + 1]:
                    z_copies[way][hop + 1][k].start()
        for way in range(2):
            more = sibling_copies(way, hop)
            for c in more:
                c.start()
            side += more
    for way in range(2):
        for hop in range(HOPS):
            for k in order[hop]:
                z_copies[way][hop][k].wait_send()
    for c in side:
        c.wait()


def ring(send, send_w, head):
    hbm = pl.BlockSpec(memory_space=pl.ANY)
    members2 = send.shape[2]
    dma = pltpu.SemaphoreType.DMA
    return pl.pallas_call(
        ring_kernel,
        out_shape=(
            jax.ShapeDtypeStruct((2 * RING, ROWS, members2), bf16),
            jax.ShapeDtypeStruct((2 * RING + STAY, ROWS, members2), bf16),
            jax.ShapeDtypeStruct((LISTS, CAPS[0], 128), f32),
            jax.ShapeDtypeStruct((LISTS + 1, CAPS[0], 128), f32),
            jax.ShapeDtypeStruct((LISTS, 8, 128), i32),
            jax.ShapeDtypeStruct((LISTS + 1, 8, 128), i32),
        ),
        in_specs=[hbm] * 3,
        out_specs=(hbm,) * 6,
        scratch_shapes=[
            dma((2, HOPS, 6)),
            dma((2, HOPS, 6)),
            dma((LISTS, 3)),
            dma((LISTS, 3)),
            dma((3,)),
            dma((3,)),
        ],
        compiler_params=pltpu.CompilerParams(collective_id=0, has_side_effects=True),
    )(send, send_w, head)


def partial_kernel(head, hm, hs, send, send_w, zm, zs, wm, ws, p, flag, v, wv, pa, pn, pw, acc, sem):
    members = pa.shape[1]
    tile = lax.axis_index("tile")
    z, core = tile // 8, tile % 2
    mine = 2 * RING + STAY
    loads = (
        (zm, v.at[pl.ds(0, 2 * RING)]),
        (send.at[pl.ds(2 * CAPS[0], STAY)], v.at[pl.ds(2 * RING, STAY)]),
        (zs, v.at[pl.ds(mine, mine)]),
        (wm, wv.at[pl.ds(0, LISTS)]),
        (send_w.at[pl.ds(2 * CAPS[0], STAY)], wv.at[LISTS, pl.ds(0, STAY)]),
        (ws, wv.at[pl.ds(LISTS + 1, LISTS + 1)]),
    )
    copies = [pltpu.make_async_copy(s, t, sem.at[i]) for i, (s, t) in enumerate(loads)]
    for c in copies:
        c.start()

    over = head[1, NR]
    for i in range(LISTS):
        over = over | hm[i, 1, NR] | hs[i, 1, NR]
    over = over | hs[LISTS, 1, NR]
    flag[...] = jnp.full(flag.shape, over, i32).astype(f32)

    expand = (lax.broadcasted_iota(i32, (256, 16), 0) // 16 == lax.broadcasted_iota(i32, (256, 16), 1)).astype(bf16)
    keep = (lax.broadcasted_iota(i32, (256, 128), 0) % 16 == lax.broadcasted_iota(i32, (256, 128), 1) % 16).astype(f32)
    pick = (lax.broadcasted_iota(i32, (8, 128), 1) // 16 == lax.broadcasted_iota(i32, (8, 128), 0)).astype(bf16)

    lists = []
    for who in range(2):
        for way in range(2):
            for hop in range(HOPS):
                entry = way * HOPS + hop
                source = hs if who else hm
                lists.append((source, entry, 0, way * NR, who * mine + hop_base(way, hop), CAPS[hop], who * (LISTS + 1) + entry))
        lists.append((hs if who else head, LISTS if who else None, 1, 0, who * mine + 2 * RING, STAY, who * (LISTS + 1) + LISTS))

    for c in copies:
        c.wait()

    def one_region(yp, carry):
        r = z * 8 + yp * 2 + core
        n = jnp.int32(0)
        for source, entry, row, shift, base, cap, wlist in lists:
            value = source[row, shift + r] if entry is None else source[entry, row, shift + r]
            start, grains = value // 256, value % 256
            grains = jnp.clip(cap - start, 0, grains)

            def gather(i, n, base=base, start=start, wlist=wlist):
                slot = start + i
                rows = pl.ds(pl.multiple_of(n * ROWS, ROWS), ROWS)
                pa[rows, :] = v[base + slot, :, 0:members]
                pn[rows, :] = v[base + slot, :, members : 2 * members]
                pw[pl.ds(n, 1), :] = wv[wlist, pl.ds(slot, 1), :]
                return n + 1

            n = lax.fori_loop(0, grains, gather, n)
        chunks = (n + 15) // 16

        def blank(i, c):
            rows = pl.ds(pl.multiple_of(i * ROWS, ROWS), ROWS)
            pa[rows, :] = jnp.zeros((ROWS, members), bf16)
            pn[rows, :] = jnp.zeros((ROWS, members), bf16)
            pw[pl.ds(i, 1), :] = jnp.zeros((1, 128), f32)
            return c

        lax.fori_loop(n, chunks * 16, blank, 0)
        acc[...] = jnp.zeros_like(acc)

        def chunk(k, c):
            rows = pl.ds(pl.multiple_of(k * 256, 256), 256)
            grains = pw[pl.ds(pl.multiple_of(k * 16, 16), 16), :].astype(bf16)
            wide = jnp.dot(expand, grains, preferred_element_type=f32) * keep
            weight = lax.dot_general(pick, wide.astype(bf16), (((1,), (1,)), ((), ())), preferred_element_type=f32)
            turned = pa[rows, :].astype(f32).T
            innovation = pn[rows, :]
            for b in range(8):
                scaled = (turned * weight[b : b + 1, :]).astype(bf16)
                acc[b] += jnp.dot(scaled, innovation, preferred_element_type=f32)
            return c

        lax.fori_loop(0, chunks, chunk, 0)
        for xp in range(NX):
            p[0, yp, xp] = acc[2 * xp].astype(bf16)
            p[1, xp, yp] = acc[2 * xp + 1].astype(bf16)
        return carry

    lax.fori_loop(0, NY, one_region, 0)


def partials(head, hm, hs, send, send_w, zm, zs, wm, ws):
    members = send.shape[2] // 2
    hbm, smem = pl.BlockSpec(memory_space=pl.ANY), pl.BlockSpec(memory_space=pltpu.SMEM)
    vmem = pl.BlockSpec(memory_space=pltpu.VMEM)
    most = 16 * 8
    return pl.pallas_call(
        partial_kernel,
        out_shape=(
            jax.ShapeDtypeStruct((2, 4, 4, members, members), bf16),
            jax.ShapeDtypeStruct((8, 128), f32),
        ),
        in_specs=[smem] * 3 + [hbm] * 6,
        out_specs=(vmem, vmem),
        scratch_shapes=[
            pltpu.VMEM((2 * (2 * RING + STAY), ROWS, 2 * members), bf16),
            pltpu.VMEM((2 * (LISTS + 1), CAPS[0], 128), f32),
            pltpu.VMEM((most * ROWS, members), bf16),
            pltpu.VMEM((most * ROWS, members), bf16),
            pltpu.VMEM((most, 128), f32),
            pltpu.VMEM((8, members, members), f32),
            pltpu.SemaphoreType.DMA((6,)),
        ],
        compiler_params=pltpu.CompilerParams(vmem_limit_bytes=48 * MIB),
    )(head, hm, hs, send, send_w, zm, zs, wm, ws)


def reduce_kernel(p, flag, total, flag_out, ro, rd, sb, u, ro2, rd2, sb2, ff, sems, recvs, fsend, frecv):
    x, tile = lax.axis_index("grp"), lax.axis_index("tile")
    z, y, core = tile // 8, (tile % 8) // 2, tile % 2

    def along(axis, step):
        if axis == 0:
            return x, z * 8 + lax.rem(y + step, NY) * 2 + core
        return lax.rem(x + step, NX), tile

    barrier = pltpu.get_barrier_semaphore()
    for axis in range(2):
        for step in (1, 3):
            pl.semaphore_signal(barrier, inc=1, device_id=along(axis, step), device_id_type=MESH)
    pl.semaphore_wait(barrier, 4)

    def copy(src, dst, half, phase, k, axis, step):
        return pltpu.make_async_remote_copy(
            src_ref=src, dst_ref=dst, send_sem=sems.at[half, phase, k], recv_sem=recvs.at[half, phase, k],
            device_id=along(axis, step), device_id_type=MESH,
        )

    def flag_copy(src, dst, k, axis, step):
        return pltpu.make_async_remote_copy(
            src_ref=ff.at[src], dst_ref=ff.at[dst], send_sem=fsend.at[k], recv_sem=frecv.at[k],
            device_id=along(axis, step), device_id_type=MESH,
        )

    ff[0] = flag[...]
    flags = [flag_copy(0, 1, 0, 0, 1), flag_copy(0, 2, 1, 0, 3)]
    for c in flags:
        c.start()

    first = []
    for half in range(2):
        me = y if half == 0 else x
        right, left, far = lax.rem(me + 1, 4), lax.rem(me + 3, 4), lax.rem(me + 2, 4)
        lo, hi = pl.ds(0, 2), pl.ds(2, 2)
        first.append([
            copy(p.at[half, far, lo], ro.at[half, 0], half, 0, 0, half, 1),
            copy(p.at[half, far, hi], ro.at[half, 1], half, 0, 1, half, 3),
            copy(p.at[half, right, hi], rd.at[half, 0, hi], half, 0, 2, half, 1),
            copy(p.at[half, left, lo], rd.at[half, 1, lo], half, 0, 3, half, 3),
            copy(sb.at[half, 0], rd.at[half, 0, lo], half, 0, 4, half, 1),
            copy(sb.at[half, 1], rd.at[half, 1, hi], half, 0, 5, half, 3),
        ])
    for k in range(4):
        for half in range(2):
            first[half][k].start()

    flags[0].wait_recv()
    ff[3] = ff[0] + ff[1]
    flags.append(flag_copy(3, 4, 2, 0, 1))
    flags[2].start()

    def wide(ref):
        return ref[...].astype(f32)

    for k in range(2):
        for half in range(2):
            me = y if half == 0 else x
            to = lax.rem(me + (1 if k == 0 else 3), 4)
            first[half][k].wait_recv()
            for i in range(2):
                sb[half, k, i] = (wide(p.at[half, to, 2 * k + i]) + wide(ro.at[half, k, i])).astype(bf16)
            first[half][4 + k].start()

    flags[1].wait_recv()
    flags[2].wait_recv()
    ff[5] = ff[0] + ff[2] + ff[4]
    flags += [flag_copy(5, 6, 3, 1, 1), flag_copy(5, 7, 4, 1, 3)]
    flags[3].start()
    flags[4].start()

    second = []
    for half in range(2):
        me, other = (y, x) if half == 0 else (x, y)
        for k in (2, 3, 4, 5):
            first[half][k].wait_recv()
        for i in range(4):
            u[half, i] = (wide(p.at[half, me, i]) + wide(rd.at[half, 0, i]) + wide(rd.at[half, 1, i])).astype(bf16)
        axis = 1 - half
        right, left, far = lax.rem(other + 1, 4), lax.rem(other + 3, 4), lax.rem(other + 2, 4)
        rows = u.shape[2] // 2
        lo, hi = pl.ds(0, rows), pl.ds(rows, rows)
        second.append([
            copy(u.at[half, far, lo], ro2.at[half, 0], half, 1, 0, axis, 1),
            copy(u.at[half, far, hi], ro2.at[half, 1], half, 1, 1, axis, 3),
            copy(u.at[half, right, hi], rd2.at[half, 0, hi], half, 1, 2, axis, 1),
            copy(u.at[half, left, lo], rd2.at[half, 1, lo], half, 1, 3, axis, 3),
            copy(sb2.at[half, 0], rd2.at[half, 0, lo], half, 1, 4, axis, 1),
            copy(sb2.at[half, 1], rd2.at[half, 1, hi], half, 1, 5, axis, 3),
        ])
        for k in range(4):
            second[half][k].start()

    flags[3].wait_recv()
    ff[8] = ff[5] + ff[6]
    flags.append(flag_copy(8, 9, 5, 1, 1))
    flags[5].start()

    for half in range(2):
        other = x if half == 0 else y
        rows = u.shape[2] // 2
        for k in range(2):
            to = lax.rem(other + (1 if k == 0 else 3), 4)
            second[half][k].wait_recv()
            sb2[half, k] = (wide(u.at[half, to, pl.ds(k * rows, rows)]) + wide(ro2.at[half, k])).astype(bf16)
            second[half][4 + k].start()

    flags[4].wait_recv()
    flags[5].wait_recv()
    flag_out[...] = ff[5] + ff[7] + ff[9]

    for half in range(2):
        other = x if half == 0 else y
        for k in (2, 3, 4, 5):
            second[half][k].wait_recv()
        total[half] = wide(u.at[half, other]) + wide(rd2.at[half, 0]) + wide(rd2.at[half, 1])

    for c in (*first[0], *first[1], *second[0], *second[1], *flags):
        c.wait_send()


def reduce_plane(p, flag):
    members = p.shape[-1]
    vmem = pl.BlockSpec(memory_space=pltpu.VMEM)
    square = (members, members)
    dma = pltpu.SemaphoreType.DMA
    return pl.pallas_call(
        reduce_kernel,
        out_shape=(jax.ShapeDtypeStruct((2, *square), f32), jax.ShapeDtypeStruct((8, 128), f32)),
        in_specs=[vmem] * 2,
        out_specs=(vmem, vmem),
        scratch_shapes=[
            pltpu.VMEM((2, 2, 2, *square), bf16),
            pltpu.VMEM((2, 2, 4, *square), bf16),
            pltpu.VMEM((2, 2, 2, *square), bf16),
            pltpu.VMEM((2, 4, *square), bf16),
            pltpu.VMEM((2, 2, members // 2, members), bf16),
            pltpu.VMEM((2, 2, *square), bf16),
            pltpu.VMEM((2, 2, members // 2, members), bf16),
            pltpu.VMEM((10, 8, 128), f32),
            dma((2, 2, 6)),
            dma((2, 2, 6)),
            dma((6,)),
            dma((6,)),
        ],
        compiler_params=pltpu.CompilerParams(collective_id=1, has_side_effects=True, vmem_limit_bytes=32 * MIB),
    )(p, flag)


def update_kernel(state, coeff, total, updated, new_coeff, coef):
    @pl.when(pl.program_id(1) == 0)
    def _():
        base = (1.0 - relaxation) * coeff[...]
        gain = relaxation * total[...]
        new_coeff[...] = base + gain
        coef[0] = base.astype(bf16)
        coef[1] = gain.astype(bf16)

    s = state[...]
    moved = jnp.dot(s, coef[0], preferred_element_type=f32) + jnp.dot(s, coef[1], preferred_element_type=f32)
    updated[...] = (s.astype(f32) + moved).astype(bf16)


def update(state, coeff, total):
    _, blocks, width, members = state.shape
    step = 1024
    square = (members, members)
    rows = pl.BlockSpec((None, None, step, members), lambda j, i: (0, j, i, 0))
    one = pl.BlockSpec((None, None, *square), lambda j, i: (0, j, 0, 0))
    return pl.pallas_call(
        update_kernel,
        grid=(blocks, width // step),
        out_shape=(jax.ShapeDtypeStruct(state.shape, bf16), jax.ShapeDtypeStruct(coeff.shape, f32)),
        in_specs=[rows, one, pl.BlockSpec((None, *square), lambda j, i: (j, 0, 0))],
        out_specs=(rows, one),
        scratch_shapes=[pltpu.VMEM((2, *square), bf16)],
        compiler_params=pltpu.CompilerParams(vmem_limit_bytes=32 * MIB),
    )(state, coeff, total)


def padded_total(obs_anom, innov, obs_rinv, obs_pos, obs_count, obs_region, obs_partner, blocks, width):
    tile_count = lax.axis_size("tile")
    nblock, observation_count, ensemble_members = obs_anom.shape
    partition_count = obs_partner.shape[1]
    nlocal = lax.axis_size("grp") * blocks
    per_neighbour = max(2, (2 * nblock + tile_count - 1) // tile_count)
    slot_count = tile_count * per_neighbour
    slot_grouping = 8
    region = obs_region[:, 0]
    order = jnp.arange(nblock, dtype=jnp.int32)
    before = (region[None, :] == region[:, None]) & (order[None, :] < order[:, None])
    destination = region * per_neighbour + jnp.sum(before.astype(jnp.int32), axis=1)
    assignment_rule = destination[None, :] == jnp.arange(slot_count, dtype=jnp.int32)[:, None]
    place_half = assignment_rule.astype(jnp.bfloat16)
    place_int = assignment_rule.astype(jnp.int32)
    labels = jnp.concatenate([obs_count[:, None], obs_partner], axis=1)
    sent_labels = jnp.dot(place_int, labels).reshape(tile_count, per_neighbour, partition_count + 1)
    stacked = jnp.concatenate([obs_anom, innov], axis=2).reshape(nblock, -1)
    packed = jnp.dot(place_half, stacked, preferred_element_type=jnp.bfloat16)
    packed = packed.reshape(tile_count, per_neighbour, observation_count, 2 * ensemble_members)
    sent_pos = jnp.dot(place_int, obs_pos).reshape(tile_count, per_neighbour, observation_count)
    sent_var = jnp.dot(assignment_rule.astype(jnp.float32), obs_rinv, precision=lax.Precision.HIGHEST)
    sent_var = sent_var.reshape(tile_count, per_neighbour, observation_count)

    def exchange(array):
        return lax.all_to_all(array, "tile", split_axis=0, concat_axis=0, tiled=True)

    received_panels = exchange(packed).reshape(slot_count, observation_count, 2 * ensemble_members)
    flattened_labels = exchange(sent_labels).reshape(slot_count, partition_count + 1)
    recv_anom = received_panels[:, :, :ensemble_members]
    recv_innov = received_panels[:, :, ensemble_members:]
    flattened_positions = exchange(sent_pos).reshape(slot_count, observation_count)
    flattened_variances = exchange(sent_var).reshape(slot_count, observation_count)
    partners = flattened_labels[:, 1:]
    block_index = jnp.arange(nlocal, dtype=jnp.int32)

    def accumulate_group(step, total):
        start = step * slot_grouping

        def part(array):
            return lax.dynamic_slice_in_dim(array, start, slot_grouping, 0)

        weights = taper_weights(
            part(flattened_positions), part(partners), part(flattened_labels)[:, 0], part(flattened_variances), width,
            ensemble_members,
        )
        scaled_part = (weights[..., None] * part(recv_innov)[:, None].astype(jnp.float32)).astype(jnp.bfloat16)
        picked = (part(partners)[..., None] == block_index).astype(jnp.bfloat16)
        by_block = jnp.einsum("qkb,qkin->qbin", picked, scaled_part, preferred_element_type=jnp.float32).astype(jnp.bfloat16)
        return total + jnp.einsum("qim,qbin->bmn", part(recv_anom), by_block, preferred_element_type=jnp.float32)

    initial_total = jnp.zeros((nlocal, ensemble_members, ensemble_members), jnp.float32)
    running_totals = lax.fori_loop(0, slot_count // slot_grouping, accumulate_group, initial_total)
    return lax.psum_scatter(running_totals.astype(jnp.bfloat16), "grp", scatter_dimension=0, tiled=True).astype(jnp.float32)


def on_device(obs_anom, innov, obs_rinv, obs_pos, obs_count, obs_region, obs_partner, state_anom, coeff):
    send, send_w, head = pack(obs_region, obs_count, obs_partner, obs_pos, obs_rinv, obs_anom, innov)
    zm, zs, wm, ws, hm, hs = ring(send, send_w, head)
    p, flag = partials(head, hm, hs, send, send_w, zm, zs, wm, ws)
    fast, flags = reduce_plane(p, flag)
    blocks, width = state_anom.shape[1:3]
    total = lax.cond(
        flags[0, 0] > 0,
        lambda *obs: padded_total(*obs[:-1], blocks, width),
        lambda *obs: obs[-1],
        obs_anom, innov, obs_rinv, obs_pos, obs_count, obs_region, obs_partner, fast,
    )
    return update(state_anom, coeff, total)


def solution(mesh):
    return jax.shard_map(
        on_device,
        mesh=mesh,
        in_specs=(
            P(("grp", "tile"), None, None),
            P(("grp", "tile"), None, None),
            P(("grp", "tile"), None),
            P(("grp", "tile"), None),
            P(("grp", "tile")),
            P(("grp", "tile"), None),
            P(("grp", "tile"), None),
            P("grp", "tile", None, None),
            P("grp", "tile", None, None),
        ),
        out_specs=(P("grp", "tile", None, None), P("grp", "tile", None, None)),
        check_vma=False,
    )
```

time: 434 us -> 171 us (0.39)
  waiting for transfers between devices: 208 us -> 0 us
  Pallas kernels: 0 us -> 141 us
  matrix products: 110 us -> 0 us
  starting transfers between devices: 33.8 us -> 0 us
  other arithmetic: 26.5 us -> 0 us
  local copies, waits for them, and re-layouts: 39.3 us -> 13.4 us
    all_to_all x4 -> x0, waiting for transfers between devices: 197 us -> none  [the longest x1 184 us: on_device(): lax.all_to_all(packed, 'tile', split_axis=0, concat_axis=0, tiled=True)]
    pallas_call x0 -> x5, Pallas kernels: none -> 141 us  [the longest x1 81.6 us: ring(): pl.pallas_call(ring_kernel, out_shape=(jax.ShapeDtypeStruct((2 * RING, RO...]
    dot_general x38 -> x0, matrix products: 110 us -> none  [the longest x16 51.4 us: accumulate_group(): jnp.einsum('qim,qbin->bmn', anom_part, by_block, preferred_element_type=j...]
    all_to_all x4 -> x0, starting transfers between devices: 33.8 us -> none  [the longest x1 12.1 us: on_device(): lax.all_to_all(sent_labels, 'tile', split_axis=0, concat_axis=0, tiled=True)]
    convert_element_type x32 -> x0, other arithmetic: 15.9 us -> none  [the longest x16 15.9 us: scaled_slice(): innov_part[:, None].astype(jnp.float32)]
    dot_general x1 -> x0, local copies, waits for them, and re-layouts: 11.4 us -> none  [on_device(): packed = jnp.dot(place_half, stacked, preferred_element_type=jnp.bfloat16)]
    reduce_scatter x1 -> x0, waiting for transfers between devices: 11.3 us -> none  [on_device(): lax.psum_scatter(running_totals.astype(jnp.bfloat16), 'grp', scatter_dime...]
    slice x18 -> x1, local copies, waits for them, and re-layouts: 7.38 us -> 0.51 us  [on_device(): flags[0, 0] > 0]
  transfers between devices with their start and end apart: 5 -> 0, of which waited for: 4 -> 0; matrix products, arithmetic and copies ran while one was open for 8% -> 0% of each run, Pallas kernels for 0% -> 0%
where the time goes in v1:
time: 171 us; the launch traced here: 169 us
  Pallas kernels  141 us (82%)
  between operations  14.8 us (9%)
  local copies, waits for them, and re-layouts  13.4 us (8%)
    pallas_call x1, Pallas kernels, ring(): pl.pallas_call(ring_kernel, out_shape=(jax.ShapeDtypeStruct((2 * RING, RO...  81.6 us
    pallas_call x1, Pallas kernels, reduce_plane(): pl.pallas_call(reduce_kernel, out_shape=(jax.ShapeDtypeStruct((2, *square...  30.3 us
    pallas_call x1, Pallas kernels, partials(): pl.pallas_call(partial_kernel, out_shape=(jax.ShapeDtypeStruct((2, 4, 4,...  17.4 us
    unnamed x38, local copies, waits for them, and re-layouts  12.9 us
    pallas_call x1, Pallas kernels, pack(): pl.pallas_call(pack_kernel, out_shape=(jax.ShapeDtypeStruct((SEND, ROWS,...  6.07 us
    pallas_call x1, Pallas kernels, update(): pl.pallas_call(update_kernel, grid=(blocks, width // step), out_shape=(ja...  5.52 us

profile of v1, /device:TPU:8, one launch (start us, length us, event | category | flops | bytes accessed | tf_op | source)
XLA Modules:
  0.0 169.3 jit_solution(17322571634920344385)
XLA Ops:
  7.2 0.7 copy.50.region
  7.9 0.8 copy.51.partner
  8.7 6.1 %shard_map.104 = (bf16[168,16,512]{2,1,0:T(8,128)(2,1)S(1)}, f32[168,128]{1,0:T(8,128)S(1)}, s32[8,128]{1,0:T(8,128)S(1)}) custom-call(s32[32,1]{1,0:T(8,128)S(1)} %copy.50.region, s32[32]{0:T(128)} %count.1, s32[32,6]{1,0:T(8,128)S(1)} %copy.51.partner, s32[32,64]{1,0:T(8,128)} %pos.1, f32[32,64]{1,0:T(8,128)} %rinv.1, bf16[32,64,256]{2,1,0:T(8,128)(2,1)} %anom.1, ...), custom_call_target="tpu_custom_call" | custom-call | tf_op jit(solution)/shard_map/pallas_call | solution.py:160
  14.7 0.0 copy-start
  14.8 1.5 copy-done
  16.3 0.6 copy-done.5
  16.9 0.6 copy-done.11
  17.5 81.6 %shard_map.105 = (bf16[380,16,512]{2,1,0:T(8,128)(2,1)}, bf16[420,16,512]{2,1,0:T(8,128)(2,1)}, f32[8,64,128]{2,1,0:T(8,128)}, f32[9,64,128]{2,1,0:T(8,128)}, s3...) custom-call(bf16[168,16,512]{2,1,0:T(8,128)(2,1)} %copy-done, f32[168,128]{1,0:T(8,128)} %copy-done.5, s32[8,128]{1,0:T(8,128)} %copy-done.11), custom_call_target="tpu_custom_call" | custom-call | tf_op jit(solution)/shard_map/pallas_call | solution.py:251
  99.1 1.0 copy-done.7
  100.1 0.9 copy-done.8
  101.0 0.8 copy-done.9
  101.8 0.8 copy-done.10
  102.5 17.4 %shard_map.106 = (bf16[2,4,4,256,256]{4,3,2,1,0:T(8,128)(2,1)}, f32[8,128]{1,0:T(8,128)S(1)}) custom-call(s32[8,128]{1,0:T(8,128)S(1)} %copy-done.12, s32[8,8,128]{2,1,0:T(8,128)S(1)} %copy-done.10, s32[9,8,128]{2,1,0:T(8,128)S(1)} %copy-done.9, bf16[168,16,512]{2,1,0:T(8,128)(2,1)S(1)} %copy-done.1, f32[168,128]{1,0:T(8,128)S(1)} %copy-done.6, ...), custom_call_target="tpu_custom_call" | custom-call | tf_op jit(solution)/shard_map/pallas_call | solution.py:369
  120.0 0.0 copy-start.3
  120.0 2.2 %copy-done.3 = bf16[2,4,4,256,256]{4,3,2,1,0:T(8,128)(2,1)S(1)} copy-done((bf16[2,4,4,256,256]{4,3,2,1,0:T(8,128)(2,1)S(1)}, bf16[2,4,4,256,256]{4,3,2,1,0:T(8,128)(2,1)}, u32[]{:S(2)}) %copy-start.3) | copy-done | bytes 4194328
  122.2 0.0 copy-start.17
  122.2 30.3 %shard_map.107 = (f32[2,256,256]{2,1,0:T(8,128)S(1)}, f32[8,128]{1,0:T(8,128)S(1)}) custom-call(bf16[2,4,4,256,256]{4,3,2,1,0:T(8,128)(2,1)S(1)} %copy-done.3, f32[8,128]{1,0:T(8,128)S(1)} %get-tuple-element.204.flag), custom_call_target="tpu_custom_call" | custom-call | tf_op jit(solution)/shard_map/pallas_call | solution.py:518
  152.5 0.5 slice.19
  153.7 0.0 copy-done.13
  153.7 0.0 copy-start.4
  153.7 0.2 conditional.1
  154.0 0.8 copy-done.4
  154.8 2.2 %copy-done.2 = bf16[1,2,4096,256]{3,2,1,0:T(8,128)(2,1)S(1)} copy-done((bf16[1,2,4096,256]{3,2,1,0:T(8,128)(2,1)S(1)}, bf16[1,2,4096,256]{3,2,1,0:T(8,128)(2,1)}, u32[]{:S(2)}) %copy-start.2) | copy-done | bytes 4194328
  157.0 5.5 %shard_map.108 = (bf16[1,2,4096,256]{3,2,1,0:T(8,128)(2,1)}, f32[1,2,256,256]{3,2,1,0:T(8,128)}) custom-call(bf16[1,2,4096,256]{3,2,1,0:T(8,128)(2,1)S(1)} %copy-done.2, f32[1,2,256,256]{3,2,1,0:T(8,128)S(1)} %copy-done.4, f32[2,256,256]{2,1,0:T(8,128)S(1)} %get-tuple-element.260.total), custom_call_target="tpu_custom_call" | custom-call | tf_op jit(solution)/shard_map/pallas_call | solution.py:561
  (21 shorter events, 0.0 us)
Async XLA Ops:
  14.7 1.5 copy-start
  16.3 0.6 copy-start.5
  16.9 0.6 copy-start.11
  17.5 81.6 %copy-start.1 = (bf16[168,16,512]{2,1,0:T(8,128)(2,1)S(1)}, bf16[168,16,512]{2,1,0:T(8,128)(2,1)}, u32[]{:S(2)}) copy-start(bf16[168,16,512]{2,1,0:T(8,128)(2,1)} %copy-done) | copy-start | bytes 8257540
  17.5 81.6 %copy-start.6 = (f32[168,128]{1,0:T(8,128)S(1)}, f32[168,128]{1,0:T(8,128)}, u32[]{:S(2)}) copy-start(f32[168,128]{1,0:T(8,128)} %copy-done.5) | copy-start | bytes 258052
  17.5 81.6 %copy-start.12 = (s32[8,128]{1,0:T(8,128)S(1)}, s32[8,128]{1,0:T(8,128)}, u32[]{:S(2)}) copy-start(s32[8,128]{1,0:T(8,128)} %copy-done.11) | copy-start | bytes 12292
  99.1 1.0 copy-start.7
  100.1 0.9 copy-start.8
  101.0 0.8 copy-start.9
  101.8 0.8 copy-start.10
  120.0 2.2 %copy-start.3 = (bf16[2,4,4,256,256]{4,3,2,1,0:T(8,128)(2,1)S(1)}, bf16[2,4,4,256,256]{4,3,2,1,0:T(8,128)(2,1)}, u32[]{:S(2)}) copy-start(bf16[2,4,4,256,256]{4,3,2,1,0:T(8,128)(2,1)} %get-tuple-element.203.p) | copy-start | bytes 12582916
  122.1 31.5 %copy-start.13 = (s32[32,64]{1,0:T(8,128)S(1)}, s32[32,64]{1,0:T(8,128)}, u32[]{:S(2)}) copy-start(s32[32,64]{1,0:T(8,128)} %pos.1) | copy-start | bytes 24580
  122.1 31.5 %copy-start.14 = (f32[32,64]{1,0:T(8,128)S(1)}, f32[32,64]{1,0:T(8,128)}, u32[]{:S(2)}) copy-start(f32[32,64]{1,0:T(8,128)} %rinv.1) | copy-start | bytes 24580
  122.1 31.5 %copy-start.15 = (s32[32,6]{0,1:T(8,128)S(1)}, s32[32,6]{0,1:T(8,128)}, u32[]{:S(2)}) copy-start(s32[32,6]{0,1:T(8,128)} %param.19) | copy-start | bytes 2308
  122.2 31.6 %copy-start.16 = (s32[32]{0:T(128)S(1)}, s32[32]{0:T(128)}, u32[]{:S(2)}) copy-start(s32[32]{0:T(128)} %count.1) | copy-start | bytes 388
  122.2 31.6 %copy-start.17 = (s32[32,1]{0,1:T(1,128)S(1)}, s32[32,1]{0,1:T(1,128)}, u32[]{:S(2)}) copy-start(s32[32,1]{0,1:T(1,128)} %param.18) | copy-start | bytes 388
  153.7 1.0 copy-start.4
  154.8 2.2 %copy-start.2 = (bf16[1,2,4096,256]{3,2,1,0:T(8,128)(2,1)S(1)}, bf16[1,2,4096,256]{3,2,1,0:T(8,128)(2,1)}, u32[]{:S(2)}) copy-start(bf16[1,2,4096,256]{3,2,1,0:T(8,128)(2,1)} %state.1) | copy-start | bytes 12582916

commit v2 on v1

v2 whole, which is shorter than its diff:
```python
import jax
import jax.numpy as jnp
from jax import lax
from jax.experimental import pallas as pl
from jax.experimental.pallas import tpu as pltpu
from jax.sharding import PartitionSpec as P

relaxation = 0.5
bf16, f32, i32 = jnp.bfloat16, jnp.float32, jnp.int32
MESH = pl.DeviceIdType.MESH
MIB = 1024 * 1024

ROWS = 16
CAPS = (64, 50, 40, 28)
STAY = 40
SEND = 2 * CAPS[0] + STAY
HOPS = len(CAPS)
NZ, NY, NX, NR = 8, 4, 4, 64
LISTS = 2 * HOPS


def taper_weights(positions, partners, counts, inverse_var, width, ensemble_members):
    center = (partners.astype(jnp.float32) + 0.5) * width
    offset = (positions.astype(jnp.float32)[..., None, :] - center[..., :, None]) / (2.0 * width)
    index = jnp.arange(positions.shape[-1], dtype=jnp.int32)
    live = index < counts[..., None]
    weight = jnp.exp(-offset * offset) * inverse_var[..., None, :] / (ensemble_members - 1.0)
    return jnp.where(live[..., None, :], weight, 0.0)


def pack_kernel(region, count, partner, pos, rinv, anom, innov, send, send_w, head, wall, size, fill, first, seat_a, seat_b):
    nblock, members = anom.shape[0], anom.shape[2]
    width = 4096.0
    z = lax.axis_index("tile") // 8

    lane = lax.broadcasted_iota(i32, (128, 128), 1)
    repeat = (lax.broadcasted_iota(i32, (128, nblock), 0) // 4 == lax.broadcasted_iota(i32, (128, nblock), 1)).astype(f32)
    column = lax.broadcasted_iota(i32, (128, 64), 1)
    quarter = (column // 16 == lax.broadcasted_iota(i32, (128, 64), 0) % 4).astype(f32)
    fold = (lax.broadcasted_iota(i32, (64, 128), 0) % 16 == lax.broadcasted_iota(i32, (64, 128), 1) % 16).astype(f32)

    def exact(a, b):
        return jnp.dot(a, b, precision=lax.Precision.HIGHEST, preferred_element_type=f32)

    def spread(values):
        return exact(exact(repeat, values) * quarter, fold)

    partners = lax.dot_general(
        repeat, partner[...].astype(f32), (((1,), (1,)), ((), ())), precision=lax.Precision.HIGHEST, preferred_element_type=f32
    )
    block_of_lane = (lane // 16).astype(f32)
    paired = jnp.zeros((128, 128), f32)
    for k in range(partner.shape[0]):
        paired = jnp.where(partners[:, k : k + 1] == block_of_lane, 1.0, paired)
    center = (block_of_lane + 0.5) * width
    offset = (spread(pos[...].astype(f32)) - center) / (2.0 * width)
    wall[...] = jnp.exp(-offset * offset) * spread(rinv[...]) / (members - 1.0) * paired

    def clear(i, c):
        size[i] = 0
        fill[i] = 0
        return c

    lax.fori_loop(0, NR, clear, 0)

    def blank(i, c):
        send[i] = jnp.zeros(send.shape[1:], bf16)
        return c

    lax.fori_loop(0, SEND, blank, 0)
    send_w[...] = jnp.zeros_like(send_w)

    def measure(o, c):
        r = region[o]
        size[r] = size[r] + (count[o] + 15) // 16
        return c

    lax.fori_loop(0, nblock, measure, 0)

    def plane(distance):
        return lax.rem(z + distance, NZ) * 8

    def total(distance):
        base = plane(distance)
        return sum(size[base + i] for i in range(8))

    d = [total(distance) for distance in range(NZ)]
    right, left = d[1] + d[2] + d[3], d[5] + d[6] + d[7]
    far_right = jnp.clip((d[4] + left - right + 1) // 2, 0, d[4])
    far_left = d[4] - far_right
    loads = (
        (right + far_right, d[2] + d[3] + far_right, d[3] + far_right, far_right),
        (left + far_left, d[6] + d[5] + far_left, d[5] + far_left, far_left),
    )
    over = (d[0] > STAY).astype(i32)
    for way in range(2):
        for hop in range(HOPS):
            over = over | (loads[way][hop] > CAPS[hop]).astype(i32)

    head_row = lax.broadcasted_iota(i32, (8, 128), 0)
    head_lane = lax.broadcasted_iota(i32, (8, 128), 1)

    def noted(header, row, at, value):
        return jnp.where((head_row == row) & (head_lane == at), value, header)

    header = noted(jnp.zeros((8, 128), i32), 1, NR, over)

    def seat_far(i, carry):
        used_right, used_left, header = carry
        r = plane(4) + i
        n = size[r]
        a = jnp.minimum(n, far_right - used_right)
        b = n - a
        header = noted(noted(header, 0, r, used_right * 256 + a), 0, NR + r, used_left * 256 + b)
        first[r] = a
        seat_a[r] = used_right
        seat_b[r] = CAPS[0] + used_left
        return used_right + a, used_left + b, header

    used_right, used_left, header = lax.fori_loop(0, 8, seat_far, (jnp.int32(0), jnp.int32(0), header))

    def seat_near(distance, base, row, shift, carry):
        def seat(i, carry):
            used, header = carry
            r = plane(distance) + i
            n = size[r]
            first[r] = n
            seat_a[r] = base + used
            seat_b[r] = base + used
            return used + n, noted(header, row, shift + r, used * 256 + n)

        return lax.fori_loop(0, 8, seat, carry)

    for distance in (3, 2, 1):
        used_right, header = seat_near(distance, 0, 0, 0, (used_right, header))
    for distance in (5, 6, 7):
        used_left, header = seat_near(distance, CAPS[0], 0, NR, (used_left, header))
    _, header = seat_near(0, 2 * CAPS[0], 1, 0, (jnp.int32(0), header))
    head[...] = header

    row_of_lane = lax.broadcasted_iota(i32, (1, 128), 1) % 16

    def place(o, c):
        r, live = region[o], count[o]
        grains = (live + 15) // 16
        start = fill[r]
        fill[r] = start + grains
        a, b, most = seat_a[r], seat_b[r], first[r]

        def one(q, c):
            f = start + q
            slot = jnp.minimum(jnp.where(f < most, a + f, b + f - most), SEND - 1)
            rows = pl.ds(pl.multiple_of(q * ROWS, ROWS), ROWS)
            send[slot, :, 0:members] = anom[o, rows, :]
            send[slot, :, members : 2 * members] = innov[o, rows, :]
            weight = wall[pl.ds(o * 4 + q, 1), :]
            send_w[pl.ds(slot, 1), :] = jnp.where(row_of_lane < live - q * ROWS, weight, 0.0)
            return c

        return lax.fori_loop(0, grains, one, c)

    lax.fori_loop(0, nblock, place, 0)


def pack(region, count, partner, pos, rinv, anom, innov):
    members = anom.shape[2]
    vmem, smem = pl.BlockSpec(memory_space=pltpu.VMEM), pl.BlockSpec(memory_space=pltpu.SMEM)
    return pl.pallas_call(
        pack_kernel,
        out_shape=(
            jax.ShapeDtypeStruct((SEND, ROWS, 2 * members), bf16),
            jax.ShapeDtypeStruct((SEND, 128), f32),
            jax.ShapeDtypeStruct((8, 128), i32),
        ),
        in_specs=[smem, smem, vmem, vmem, vmem, vmem, vmem],
        out_specs=(vmem, vmem, vmem),
        scratch_shapes=[pltpu.VMEM((128, 128), f32)] + [pltpu.SMEM((NR,), i32)] * 5,
        compiler_params=pltpu.CompilerParams(vmem_limit_bytes=16 * MIB),
    )(region, count, partner, pos, rinv, anom, innov)


def exchange_kernel(send, send_w, head, total, flag_out, *scratch):
    scratch = list(scratch)

    def take(n):
        out = scratch[:n]
        del scratch[:n]
        return out

    zm, zs, wm, ws = take(LISTS), take(LISTS + 1), take(LISTS), take(LISTS + 1)
    hm, hs, hsm, pa, pn, pw, acc, p, ro, rd, sb, u, ro2, rd2, sb2, ff = take(16)
    zsend, zrecv, ssend, srecv, osend, orecv, hsem, sems, recvs, fsend, frecv = take(11)

    members = pa.shape[1]
    x, tile = lax.axis_index("grp"), lax.axis_index("tile")
    z, inner = tile // 8, tile % 8
    y, core = inner // 2, inner % 2
    sibling = tile + 1 - 2 * core

    def around(step):
        return x, lax.rem(z + step, NZ) * 8 + inner

    def along(axis, step):
        if axis == 0:
            return x, z * 8 + lax.rem(y + step, NY) * 2 + core
        return lax.rem(x + step, NX), tile

    ways = (around(1), around(NZ - 1))
    barrier = pltpu.get_barrier_semaphore()
    for other in (*ways, (x, sibling), along(0, 1), along(0, 3), along(1, 1), along(1, 3)):
        pl.semaphore_signal(barrier, inc=1, device_id=other, device_id_type=MESH)
    pl.semaphore_wait(barrier, 7)

    def copy(src, dst, send_sem, recv_sem, other):
        return pltpu.make_async_remote_copy(
            src_ref=src, dst_ref=dst, send_sem=send_sem, recv_sem=recv_sem, device_id=other, device_id_type=MESH
        )

    edges = (0, *CAPS[::-1])

    def hop_copies(way, hop):
        entry = way * HOPS + hop
        out = []
        for k in range(HOPS - hop):
            lo, n = edges[k], edges[k + 1] - edges[k]
            src = send.at[pl.ds(way * CAPS[0] + lo, n)] if hop == 0 else zm[entry - 1].at[pl.ds(lo, n)]
            out.append((k, src, zm[entry].at[pl.ds(lo, n)]))
        out.append((4, send_w.at[pl.ds(way * CAPS[0], CAPS[0])] if hop == 0 else wm[entry - 1], wm[entry]))
        out.append((5, head if hop == 0 else hm.at[entry - 1], hm.at[entry]))
        return {k: copy(src, dst, zsend.at[way, hop, k], zrecv.at[way, hop, k], ways[way]) for k, src, dst in out}

    z_copies = [[hop_copies(way, hop) for hop in range(HOPS)] for way in range(2)]
    order = [[5, 4, *range(HOPS - hop)] for hop in range(HOPS)]
    side = [
        [copy(s, t, ssend.at[e, i], srecv.at[e, i], (x, sibling)) for i, (s, t) in enumerate(
            ((hm.at[e], hs.at[e]), (zm[e], zs[e]), (wm[e], ws[e])))]
        for e in range(LISTS)
    ]
    stay = pl.ds(2 * CAPS[0], STAY)
    side.append([
        copy(head, hs.at[LISTS], osend.at[0], orecv.at[0], (x, sibling)),
        copy(send.at[stay], zs[LISTS], osend.at[1], orecv.at[1], (x, sibling)),
        copy(send_w.at[stay], ws[LISTS], osend.at[2], orecv.at[2], (x, sibling)),
    ])
    to_scalar = [pltpu.make_async_copy(hm.at[e], hsm.at[e], hsem.at[e]) for e in range(LISTS)]
    to_scalar.append(pltpu.make_async_copy(head, hsm.at[LISTS], hsem.at[LISTS]))
    to_scalar += [pltpu.make_async_copy(hs.at[e], hsm.at[LISTS + 1 + e], hsem.at[LISTS + 1 + e]) for e in range(LISTS + 1)]

    for k in order[0]:
        for way in range(2):
            z_copies[way][0][k].start()
    for c in side[LISTS]:
        c.start()
    to_scalar[LISTS].start()

    expand = (lax.broadcasted_iota(i32, (256, 16), 0) // 16 == lax.broadcasted_iota(i32, (256, 16), 1)).astype(bf16)
    keep = (lax.broadcasted_iota(i32, (256, 128), 0) % 16 == lax.broadcasted_iota(i32, (256, 128), 1) % 16).astype(f32)
    pick = (lax.broadcasted_iota(i32, (8, 128), 1) // 16 == lax.broadcasted_iota(i32, (8, 128), 0)).astype(bf16)

    def accumulate(entry, row, shift, cap, mode):
        own = entry == LISTS
        halves = (
            (send if own else zm[entry], send_w if own else wm[entry], entry, 2 * CAPS[0] if own else 0),
            (zs[entry], ws[entry], LISTS + 1 + entry, 0),
        )

        def one_region(yp, carry):
            r = z * 8 + yp * 2 + core
            for half, (panels, weights, at, base) in enumerate(halves):
                value = hsm[at, row, shift + r]
                start, grains = value // 256, value % 256
                for i in range(8):
                    slot = base + jnp.minimum(start + i, cap - 1)
                    rows = pl.ds(half * 128 + i * ROWS, ROWS)
                    pa[rows, :] = panels[slot, :, 0:members]
                    pn[rows, :] = panels[slot, :, members : 2 * members]
                    pw[pl.ds(half * 8 + i, 1), :] = jnp.where(i < grains, weights[pl.ds(slot, 1), :], 0.0)
            wide = jnp.dot(expand, pw[...].astype(bf16), preferred_element_type=f32) * keep
            weight = lax.dot_general(pick, wide.astype(bf16), (((1,), (1,)), ((), ())), preferred_element_type=f32)
            turned = pa[...].astype(f32).T
            innovation = pn[...]
            for b in range(8):
                scaled = (turned * weight[b : b + 1, :]).astype(bf16)
                product = jnp.dot(scaled, innovation, preferred_element_type=f32)
                if mode == 0:
                    acc[yp, b] = product
                elif mode == 1:
                    acc[yp, b] += product
                elif b % 2 == 0:
                    p[0, yp, b // 2] = (acc[yp, b] + product).astype(bf16)
                else:
                    p[1, b // 2, yp] = (acc[yp, b] + product).astype(bf16)
            return carry

        lax.fori_loop(0, NY, one_region, 0)

    def ready(entry):
        for c in side[entry]:
            c.wait_recv()
        for at in (entry, LISTS + 1 + entry):
            if at > LISTS:
                to_scalar[at].start()
            to_scalar[at].wait()

    for hop in range(HOPS):
        for k in order[hop]:
            for way in range(2):
                entry = way * HOPS + hop
                z_copies[way][hop][k].wait_recv()
                if k in z_copies[way][min(hop + 1, HOPS - 1)] and hop + 1 < HOPS:
                    z_copies[way][hop + 1][k].start()
                if k == 5:
                    side[entry][0].start()
                    to_scalar[entry].start()
        for way in range(2):
            entry = way * HOPS + hop
            side[entry][1].start()
            side[entry][2].start()
        if hop == 0:
            ready(LISTS)
            accumulate(LISTS, 1, 0, STAY, 0)
        else:
            for way in range(2):
                ready(way * HOPS + hop - 1)
                accumulate(way * HOPS + hop - 1, 0, way * NR, CAPS[hop - 1], 1)
    for way in range(2):
        ready(way * HOPS + HOPS - 1)
        accumulate(way * HOPS + HOPS - 1, 0, way * NR, CAPS[HOPS - 1], 1 + way)

    def half_copy(src, dst, half, phase, k, axis, step):
        return copy(src, dst, sems.at[half, phase, k], recvs.at[half, phase, k], along(axis, step))

    first = []
    for half in range(2):
        me = y if half == 0 else x
        right, left, far = lax.rem(me + 1, 4), lax.rem(me + 3, 4), lax.rem(me + 2, 4)
        lo, hi = pl.ds(0, 2), pl.ds(2, 2)
        first.append([
            half_copy(p.at[half, far, lo], ro.at[half, 0], half, 0, 0, half, 1),
            half_copy(p.at[half, far, hi], ro.at[half, 1], half, 0, 1, half, 3),
            half_copy(p.at[half, right, hi], rd.at[half, 0, hi], half, 0, 2, half, 1),
            half_copy(p.at[half, left, lo], rd.at[half, 1, lo], half, 0, 3, half, 3),
            half_copy(sb.at[half, 0], rd.at[half, 0, lo], half, 0, 4, half, 1),
            half_copy(sb.at[half, 1], rd.at[half, 1, hi], half, 0, 5, half, 3),
        ])
    for k in range(4):
        for half in range(2):
            first[half][k].start()

    def flag_copy(src, dst, k, axis, step):
        return copy(ff.at[src], ff.at[dst], fsend.at[k], frecv.at[k], along(axis, step))

    flag = head[...] + hs[LISTS]
    for e in range(LISTS):
        flag = flag + hm[e] + hs[e]
    ff[0] = flag.astype(f32)
    flags = [flag_copy(0, 1, 0, 0, 1), flag_copy(0, 2, 1, 0, 3)]
    for c in flags:
        c.start()
    flags[0].wait_recv()
    ff[3] = ff[0] + ff[1]
    flags.append(flag_copy(3, 4, 2, 0, 1))
    flags[2].start()

    def wide_of(ref):
        return ref[...].astype(f32)

    for k in range(2):
        for half in range(2):
            me = y if half == 0 else x
            to = lax.rem(me + (1 if k == 0 else 3), 4)
            first[half][k].wait_recv()
            for i in range(2):
                sb[half, k, i] = (wide_of(p.at[half, to, 2 * k + i]) + wide_of(ro.at[half, k, i])).astype(bf16)
            first[half][4 + k].start()

    flags[1].wait_recv()
    flags[2].wait_recv()
    ff[5] = ff[0] + ff[2] + ff[4]
    flags += [flag_copy(5, 6, 3, 1, 1), flag_copy(5, 7, 4, 1, 3)]
    flags[3].start()
    flags[4].start()

    second = []
    for half in range(2):
        me, other = (y, x) if half == 0 else (x, y)
        for k in (2, 3, 4, 5):
            first[half][k].wait_recv()
        for i in range(4):
            u[half, i] = (wide_of(p.at[half, me, i]) + wide_of(rd.at[half, 0, i]) + wide_of(rd.at[half, 1, i])).astype(bf16)
        axis = 1 - half
        right, left, far = lax.rem(other + 1, 4), lax.rem(other + 3, 4), lax.rem(other + 2, 4)
        rows = u.shape[2] // 2
        lo, hi = pl.ds(0, rows), pl.ds(rows, rows)
        second.append([
            half_copy(u.at[half, far, lo], ro2.at[half, 0], half, 1, 0, axis, 1),
            half_copy(u.at[half, far, hi], ro2.at[half, 1], half, 1, 1, axis, 3),
            half_copy(u.at[half, right, hi], rd2.at[half, 0, hi], half, 1, 2, axis, 1),
            half_copy(u.at[half, left, lo], rd2.at[half, 1, lo], half, 1, 3, axis, 3),
            half_copy(sb2.at[half, 0], rd2.at[half, 0, lo], half, 1, 4, axis, 1),
            half_copy(sb2.at[half, 1], rd2.at[half, 1, hi], half, 1, 5, axis, 3),
        ])
        for k in range(4):
            second[half][k].start()

    flags[3].wait_recv()
    ff[8] = ff[5] + ff[6]
    flags.append(flag_copy(8, 9, 5, 1, 1))
    flags[5].start()

    for half in range(2):
        other = x if half == 0 else y
        rows = u.shape[2] // 2
        for k in range(2):
            to = lax.rem(other + (1 if k == 0 else 3), 4)
            second[half][k].wait_recv()
            sb2[half, k] = (wide_of(u.at[half, to, pl.ds(k * rows, rows)]) + wide_of(ro2.at[half, k])).astype(bf16)
            second[half][4 + k].start()

    flags[4].wait_recv()
    flags[5].wait_recv()
    flag_out[...] = ff[5] + ff[7] + ff[9]

    for half in range(2):
        other = x if half == 0 else y
        for k in (2, 3, 4, 5):
            second[half][k].wait_recv()
        total[half] = wide_of(u.at[half, other]) + wide_of(rd2.at[half, 0]) + wide_of(rd2.at[half, 1])

    for way in range(2):
        for hop in range(HOPS):
            for k in order[hop]:
                z_copies[way][hop][k].wait_send()
    for group in side:
        for c in group:
            c.wait_send()
    for c in (*first[0], *first[1], *second[0], *second[1], *flags):
        c.wait_send()


def exchange(send, send_w, head):
    vmem = pl.BlockSpec(memory_space=pltpu.VMEM)
    members = send.shape[2] // 2
    square = (members, members)
    dma = pltpu.SemaphoreType.DMA
    panels = [pltpu.VMEM((cap, ROWS, 2 * members), bf16) for cap in CAPS] * 2
    weights = [pltpu.VMEM((CAPS[0], 128), f32)] * LISTS
    return pl.pallas_call(
        exchange_kernel,
        out_shape=(jax.ShapeDtypeStruct((2, *square), f32), jax.ShapeDtypeStruct((8, 128), f32)),
        in_specs=[vmem] * 3,
        out_specs=(vmem, vmem),
        scratch_shapes=[
            *panels,
            *panels,
            pltpu.VMEM((STAY, ROWS, 2 * members), bf16),
            *weights,
            *weights,
            pltpu.VMEM((STAY, 128), f32),
            pltpu.VMEM((LISTS, 8, 128), i32),
            pltpu.VMEM((LISTS + 1, 8, 128), i32),
            pltpu.SMEM((2 * LISTS + 2, 8, 128), i32),
            pltpu.VMEM(square, bf16),
            pltpu.VMEM(square, bf16),
            pltpu.VMEM((16, 128), f32),
            pltpu.VMEM((4, 8, *square), f32),
            pltpu.VMEM((2, 4, 4, *square), bf16),
            pltpu.VMEM((2, 2, 2, *square), bf16),
            pltpu.VMEM((2, 2, 4, *square), bf16),
            pltpu.VMEM((2, 2, 2, *square), bf16),
            pltpu.VMEM((2, 4, *square), bf16),
            pltpu.VMEM((2, 2, members // 2, members), bf16),
            pltpu.VMEM((2, 2, *square), bf16),
            pltpu.VMEM((2, 2, members // 2, members), bf16),
            pltpu.VMEM((10, 8, 128), f32),
            dma((2, HOPS, 6)),
            dma((2, HOPS, 6)),
            dma((LISTS, 3)),
            dma((LISTS, 3)),
            dma((3,)),
            dma((3,)),
            dma((2 * LISTS + 2,)),
            dma((2, 2, 6)),
            dma((2, 2, 6)),
            dma((6,)),
            dma((6,)),
        ],
        compiler_params=pltpu.CompilerParams(collective_id=0, has_side_effects=True, vmem_limit_bytes=46 * MIB),
    )(send, send_w, head)


def update_kernel(state, coeff, total, updated, new_coeff, coef):
    @pl.when(pl.program_id(1) == 0)
    def _():
        base = (1.0 - relaxation) * coeff[...]
        gain = relaxation * total[...]
        new_coeff[...] = base + gain
        coef[0] = base.astype(bf16)
        coef[1] = gain.astype(bf16)

    s = state[...]
    moved = jnp.dot(s, coef[0], preferred_element_type=f32) + jnp.dot(s, coef[1], preferred_element_type=f32)
    updated[...] = (s.astype(f32) + moved).astype(bf16)


def update(state, coeff, total):
    _, blocks, width, members = state.shape
    step = 2048
    square = (members, members)
    rows = pl.BlockSpec((None, None, step, members), lambda j, i: (0, j, i, 0))
    one = pl.BlockSpec((None, None, *square), lambda j, i: (0, j, 0, 0))
    return pl.pallas_call(
        update_kernel,
        grid=(blocks, width // step),
        out_shape=(jax.ShapeDtypeStruct(state.shape, bf16), jax.ShapeDtypeStruct(coeff.shape, f32)),
        in_specs=[rows, one, pl.BlockSpec((None, *square), lambda j, i: (j, 0, 0))],
        out_specs=(rows, one),
        scratch_shapes=[pltpu.VMEM((2, *square), bf16)],
        compiler_params=pltpu.CompilerParams(vmem_limit_bytes=16 * MIB),
    )(state, coeff, total)


def padded_total(obs_anom, innov, obs_rinv, obs_pos, obs_count, obs_region, obs_partner, blocks, width):
    tile_count = lax.axis_size("tile")
    nblock, observation_count, ensemble_members = obs_anom.shape
    partition_count = obs_partner.shape[1]
    nlocal = lax.axis_size("grp") * blocks
    per_neighbour = max(2, (2 * nblock + tile_count - 1) // tile_count)
    slot_count = tile_count * per_neighbour
    slot_grouping = 8
    region = obs_region[:, 0]
    order = jnp.arange(nblock, dtype=jnp.int32)
    before = (region[None, :] == region[:, None]) & (order[None, :] < order[:, None])
    destination = region * per_neighbour + jnp.sum(before.astype(jnp.int32), axis=1)
    assignment_rule = destination[None, :] == jnp.arange(slot_count, dtype=jnp.int32)[:, None]
    place_half = assignment_rule.astype(jnp.bfloat16)
    place_int = assignment_rule.astype(jnp.int32)
    labels = jnp.concatenate([obs_count[:, None], obs_partner], axis=1)
    sent_labels = jnp.dot(place_int, labels).reshape(tile_count, per_neighbour, partition_count + 1)
    stacked = jnp.concatenate([obs_anom, innov], axis=2).reshape(nblock, -1)
    packed = jnp.dot(place_half, stacked, preferred_element_type=jnp.bfloat16)
    packed = packed.reshape(tile_count, per_neighbour, observation_count, 2 * ensemble_members)
    sent_pos = jnp.dot(place_int, obs_pos).reshape(tile_count, per_neighbour, observation_count)
    sent_var = jnp.dot(assignment_rule.astype(jnp.float32), obs_rinv, precision=lax.Precision.HIGHEST)
    sent_var = sent_var.reshape(tile_count, per_neighbour, observation_count)

    def exchange(array):
        return lax.all_to_all(array, "tile", split_axis=0, concat_axis=0, tiled=True)

    received_panels = exchange(packed).reshape(slot_count, observation_count, 2 * ensemble_members)
    flattened_labels = exchange(sent_labels).reshape(slot_count, partition_count + 1)
    recv_anom = received_panels[:, :, :ensemble_members]
    recv_innov = received_panels[:, :, ensemble_members:]
    flattened_positions = exchange(sent_pos).reshape(slot_count, observation_count)
    flattened_variances = exchange(sent_var).reshape(slot_count, observation_count)
    partners = flattened_labels[:, 1:]
    block_index = jnp.arange(nlocal, dtype=jnp.int32)

    def accumulate_group(step, total):
        start = step * slot_grouping

        def part(array):
            return lax.dynamic_slice_in_dim(array, start, slot_grouping, 0)

        weights = taper_weights(
            part(flattened_positions), part(partners), part(flattened_labels)[:, 0], part(flattened_variances), width,
            ensemble_members,
        )
        scaled_part = (weights[..., None] * part(recv_innov)[:, None].astype(jnp.float32)).astype(jnp.bfloat16)
        picked = (part(partners)[..., None] == block_index).astype(jnp.bfloat16)
        by_block = jnp.einsum("qkb,qkin->qbin", picked, scaled_part, preferred_element_type=jnp.float32).astype(jnp.bfloat16)
        return total + jnp.einsum("qim,qbin->bmn", part(recv_anom), by_block, preferred_element_type=jnp.float32)

    initial_total = jnp.zeros((nlocal, ensemble_members, ensemble_members), jnp.float32)
    running_totals = lax.fori_loop(0, slot_count // slot_grouping, accumulate_group, initial_total)
    return lax.psum_scatter(running_totals.astype(jnp.bfloat16), "grp", scatter_dimension=0, tiled=True).astype(jnp.float32)


def on_device(obs_anom, innov, obs_rinv, obs_pos, obs_count, obs_region, obs_partner, state_anom, coeff):
    send, send_w, head = pack(obs_region[:, 0], obs_count, obs_partner.T, obs_pos, obs_rinv, obs_anom, innov)
    fast, flags = exchange(send, send_w, head)
    blocks, width = state_anom.shape[1:3]
    total = lax.cond(
        flags[1, NR] > 0,
        lambda *obs: padded_total(*obs[:-1], blocks, width),
        lambda *obs: obs[-1],
        obs_anom, innov, obs_rinv, obs_pos, obs_count, obs_region, obs_partner, fast,
    )
    return update(state_anom, coeff, total)


def solution(mesh):
    return jax.shard_map(
        on_device,
        mesh=mesh,
        in_specs=(
            P(("grp", "tile"), None, None),
            P(("grp", "tile"), None, None),
            P(("grp", "tile"), None),
            P(("grp", "tile"), None),
            P(("grp", "tile")),
            P(("grp", "tile"), None),
            P(("grp", "tile"), None),
            P("grp", "tile", None, None),
            P("grp", "tile", None, None),
        ),
        out_specs=(P("grp", "tile", None, None), P("grp", "tile", None, None)),
        check_vma=False,
    )
```

time: 171 us -> 150 us (0.88); the launches traced: 169 us -> 150 us
  local copies, waits for them, and re-layouts: 13.4 us -> 3.59 us
  Pallas kernels: 141 us -> 132 us
    unnamed x38 -> x14, local copies, waits for them, and re-layouts: 12.9 us -> 3.01 us
    pallas_call x3 -> x1, Pallas kernels: 129 us -> 121 us  [exchange(): pl.pallas_call(exchange_kernel, out_shape=(jax.ShapeDtypeStruct((2, *squa...]
where the time goes in v2:
time: 150 us
  Pallas kernels  132 us (88%)
  between operations  14.8 us (10%)
  local copies, waits for them, and re-layouts  3.59 us (2%)
    pallas_call x1, Pallas kernels, exchange(): pl.pallas_call(exchange_kernel, out_shape=(jax.ShapeDtypeStruct((2, *squa...  121 us
    pallas_call x1, Pallas kernels, pack(): pl.pallas_call(pack_kernel, out_shape=(jax.ShapeDtypeStruct((SEND, ROWS,...  6.25 us
    pallas_call x1, Pallas kernels, update(): pl.pallas_call(update_kernel, grid=(blocks, width // step), out_shape=(ja...  4.24 us
    unnamed x14, local copies, waits for them, and re-layouts  3.01 us

profile of v2, /device:TPU:8, one launch (start us, length us, event | category | flops | bytes accessed | tf_op | source)
XLA Modules:
  0.0 150.2 jit_solution(16998409404070026400)
XLA Ops:
  7.2 0.0 copy-start.2
  7.2 0.0 copy-start.3
  7.2 0.0 copy-start.4
  7.2 0.0 copy-start.5
  7.2 0.0 copy-start.6
  7.2 6.2 %shard_map.104 = (bf16[168,16,512]{2,1,0:T(8,128)(2,1)S(1)}, f32[168,128]{1,0:T(8,128)S(1)}, s32[8,128]{1,0:T(8,128)S(1)}) custom-call(s32[32]{0:T(128)} %bitcast.70, s32[32]{0:T(128)} %count.1, s32[6,32]{1,0:T(8,128)} %bitcast.67, s32[32,64]{1,0:T(8,128)} %pos.1, f32[32,64]{1,0:T(8,128)} %rinv.1, bf16[32,64,256]{2,1,0:T(8,128)(2,1)} %anom.1, ...), custom_call_target="tpu_custom_call" | custom-call | tf_op jit(solution)/shard_map/pallas_call | solution.py:168
  13.5 121.2 %shard_map.105 = (f32[2,256,256]{2,1,0:T(8,128)S(1)}, f32[8,128]{1,0:T(8,128)S(1)}) custom-call(bf16[168,16,512]{2,1,0:T(8,128)(2,1)S(1)} %get-tuple-element.186.send, f32[168,128]{1,0:T(8,128)S(1)} %get-tuple-element.187.send_w, s32[8,128]{1,0:T(8,128)S(1)} %get-tuple-element.188.head), custom_call_target="tpu_custom_call" | custom-call | tf_op jit(solution)/shard_map/pallas_call | solution.py:448
  134.6 0.6 slice.19
  135.9 0.0 copy-done.2
  135.9 0.0 copy-done.3
  135.9 0.0 copy-done.4
  135.9 0.0 copy-done.5
  135.9 0.0 copy-done.6
  135.9 0.0 copy-start.1
  135.9 0.2 conditional.1
  136.2 0.8 copy-done.1
  137.0 0.0 copy-start
  137.0 2.2 %copy-done = bf16[1,2,4096,256]{3,2,1,0:T(8,128)(2,1)S(1)} copy-done((bf16[1,2,4096,256]{3,2,1,0:T(8,128)(2,1)S(1)}, bf16[1,2,4096,256]{3,2,1,0:T(8,128)(2,1)}, u32[]{:S(2)}) %copy-start) | copy-done | bytes 4194328
  139.2 4.2 %shard_map.106 = (bf16[1,2,4096,256]{3,2,1,0:T(8,128)(2,1)}, f32[1,2,256,256]{3,2,1,0:T(8,128)}) custom-call(bf16[1,2,4096,256]{3,2,1,0:T(8,128)(2,1)S(1)} %copy-done, f32[1,2,256,256]{3,2,1,0:T(8,128)S(1)} %copy-done.1, f32[2,256,256]{2,1,0:T(8,128)S(1)} %get-tuple-element.244.total), custom_call_target="tpu_custom_call" | custom-call | tf_op jit(solution)/shard_map/pallas_call | solution.py:512
Async XLA Ops:
  7.2 128.7 %copy-start.2 = (s32[32,64]{1,0:T(8,128)S(1)}, s32[32,64]{1,0:T(8,128)}, u32[]{:S(2)}) copy-start(s32[32,64]{1,0:T(8,128)} %pos.1) | copy-start | bytes 24580
  7.2 128.7 %copy-start.3 = (f32[32,64]{1,0:T(8,128)S(1)}, f32[32,64]{1,0:T(8,128)}, u32[]{:S(2)}) copy-start(f32[32,64]{1,0:T(8,128)} %rinv.1) | copy-start | bytes 24580
  7.2 128.7 %copy-start.4 = (s32[32,6]{0,1:T(8,128)S(1)}, s32[32,6]{0,1:T(8,128)}, u32[]{:S(2)}) copy-start(s32[32,6]{0,1:T(8,128)} %param.19) | copy-start | bytes 2308
  7.2 128.7 %copy-start.5 = (s32[32]{0:T(128)S(1)}, s32[32]{0:T(128)}, u32[]{:S(2)}) copy-start(s32[32]{0:T(128)} %count.1) | copy-start | bytes 388
  7.2 128.7 %copy-start.6 = (s32[32,1]{0,1:T(1,128)S(1)}, s32[32,1]{0,1:T(1,128)}, u32[]{:S(2)}) copy-start(s32[32,1]{0,1:T(1,128)} %param.18) | copy-start | bytes 388
  135.9 1.0 copy-start.1
  137.0 2.2 %copy-start = (bf16[1,2,4096,256]{3,2,1,0:T(8,128)(2,1)S(1)}, bf16[1,2,4096,256]{3,2,1,0:T(8,128)(2,1)}, u32[]{:S(2)}) copy-start(bf16[1,2,4096,256]{3,2,1,0:T(8,128)(2,1)} %state.1) | copy-start | bytes 12582916

commit v3 on v2

v3 whole, which is shorter than its diff:
```python
import jax
import jax.numpy as jnp
from jax import lax
from jax.experimental import pallas as pl
from jax.experimental.pallas import tpu as pltpu
from jax.sharding import PartitionSpec as P

relaxation = 0.5
bf16, f32, i32 = jnp.bfloat16, jnp.float32, jnp.int32
MESH = pl.DeviceIdType.MESH
MIB = 1024 * 1024

ROWS = 16
CAPS = (64, 50, 40, 28)
STAY = 40
SEND = 2 * CAPS[0] + STAY
HOPS = len(CAPS)
NZ, NY, NX, NR = 8, 4, 4, 64
LISTS = 2 * HOPS
HALF = 128
WCAPS = tuple((cap + 7) // 8 * 8 for cap in CAPS)
STAGES = 2 * HOPS


def taper_weights(positions, partners, counts, inverse_var, width, ensemble_members):
    center = (partners.astype(jnp.float32) + 0.5) * width
    offset = (positions.astype(jnp.float32)[..., None, :] - center[..., :, None]) / (2.0 * width)
    index = jnp.arange(positions.shape[-1], dtype=jnp.int32)
    live = index < counts[..., None]
    weight = jnp.exp(-offset * offset) * inverse_var[..., None, :] / (ensemble_members - 1.0)
    return jnp.where(live[..., None, :], weight, 0.0)


def pack_kernel(region, count, partner, pos, rinv, anom, innov, send, send_b, send_w, head, wall, held, size, fill, first, seat_a, seat_b, sem):
    nblock, members = anom.shape[0], anom.shape[2]
    width = 4096.0
    z = lax.axis_index("tile") // 8
    loads = [pltpu.make_async_copy(source, held.at[i], sem.at[i]) for i, source in enumerate((anom, innov))]
    for c in loads:
        c.start()

    lane = lax.broadcasted_iota(i32, (128, 128), 1)
    repeat = (lax.broadcasted_iota(i32, (128, nblock), 0) // 4 == lax.broadcasted_iota(i32, (128, nblock), 1)).astype(f32)
    column = lax.broadcasted_iota(i32, (128, 64), 1)
    quarter = (column // 16 == lax.broadcasted_iota(i32, (128, 64), 0) % 4).astype(f32)
    fold = (lax.broadcasted_iota(i32, (64, 128), 0) % 16 == lax.broadcasted_iota(i32, (64, 128), 1) % 16).astype(f32)

    def exact(a, b):
        return jnp.dot(a, b, precision=lax.Precision.HIGHEST, preferred_element_type=f32)

    def spread(values):
        return exact(exact(repeat, values) * quarter, fold)

    partners = lax.dot_general(
        repeat, partner[...].astype(f32), (((1,), (1,)), ((), ())), precision=lax.Precision.HIGHEST, preferred_element_type=f32
    )
    block_of_lane = (lane // 16).astype(f32)
    paired = jnp.zeros((128, 128), f32)
    for k in range(partner.shape[0]):
        paired = jnp.where(partners[:, k : k + 1] == block_of_lane, 1.0, paired)
    center = (block_of_lane + 0.5) * width
    offset = (spread(pos[...].astype(f32)) - center) / (2.0 * width)
    wall[...] = jnp.exp(-offset * offset) * spread(rinv[...]) / (members - 1.0) * paired

    def clear(i, c):
        size[i] = 0
        fill[i] = 0
        return c

    lax.fori_loop(0, NR, clear, 0)

    def blank(i, c):
        send[i] = jnp.zeros(send.shape[1:], bf16)
        send_b[i] = jnp.zeros(send_b.shape[1:], bf16)
        return c

    lax.fori_loop(0, SEND, blank, 0)
    send_w[...] = jnp.zeros_like(send_w)

    def measure(o, c):
        r = region[o]
        size[r] = size[r] + (count[o] + 15) // 16
        return c

    lax.fori_loop(0, nblock, measure, 0)

    def plane(distance):
        return lax.rem(z + distance, NZ) * 8

    def total(distance):
        base = plane(distance)
        return sum(size[base + i] for i in range(8))

    d = [total(distance) for distance in range(NZ)]
    right, left = d[1] + d[2] + d[3], d[5] + d[6] + d[7]
    far_right = jnp.clip((d[4] + left - right + 1) // 2, 0, d[4])
    far_left = d[4] - far_right
    counts = (
        (right + far_right, d[2] + d[3] + far_right, d[3] + far_right, far_right),
        (left + far_left, d[6] + d[5] + far_left, d[5] + far_left, far_left),
    )
    over = (d[0] > STAY).astype(i32)
    for way in range(2):
        for hop in range(HOPS):
            over = over | (counts[way][hop] > CAPS[hop]).astype(i32)

    head_row = lax.broadcasted_iota(i32, (8, 128), 0)
    head_lane = lax.broadcasted_iota(i32, (8, 128), 1)

    def noted(header, row, at, value):
        return jnp.where((head_row == row) & (head_lane == at), value, header)

    header = noted(jnp.zeros((8, 128), i32), 1, NR, over)

    def seat_far(i, carry):
        used_right, used_left, header = carry
        r = plane(4) + i
        n = size[r]
        a = jnp.minimum(n, far_right - used_right)
        b = n - a
        header = noted(noted(header, 0, r, used_right * 256 + a), 0, NR + r, used_left * 256 + b)
        first[r] = a
        seat_a[r] = used_right
        seat_b[r] = CAPS[0] + used_left
        return used_right + a, used_left + b, header

    used_right, used_left, header = lax.fori_loop(0, 8, seat_far, (jnp.int32(0), jnp.int32(0), header))

    def seat_near(distance, base, row, shift, carry):
        def seat(i, carry):
            used, header = carry
            r = plane(distance) + i
            n = size[r]
            first[r] = n
            seat_a[r] = base + used
            seat_b[r] = base + used
            return used + n, noted(header, row, shift + r, used * 256 + n)

        return lax.fori_loop(0, 8, seat, carry)

    for distance in (3, 2, 1):
        used_right, header = seat_near(distance, 0, 0, 0, (used_right, header))
    for distance in (5, 6, 7):
        used_left, header = seat_near(distance, CAPS[0], 0, NR, (used_left, header))
    _, header = seat_near(0, 2 * CAPS[0], 1, 0, (jnp.int32(0), header))
    head[...] = header
    for c in loads:
        c.wait()

    row_of_lane = lax.broadcasted_iota(i32, (1, 128), 1) % 16

    def place(o, c):
        r, live = region[o], count[o]
        grains = (live + 15) // 16
        start = fill[r]
        fill[r] = start + grains
        a, b, most = seat_a[r], seat_b[r], first[r]

        def one(q, c):
            f = start + q
            slot = jnp.minimum(jnp.where(f < most, a + f, b + f - most), SEND - 1)
            rows = pl.ds(pl.multiple_of(q * ROWS, ROWS), ROWS)
            send[slot, :, 0:members] = held[0, o, rows, :]
            send[slot, :, members : members + HALF] = held[1, o, rows, 0:HALF]
            send_b[slot] = held[1, o, rows, HALF:members]
            weight = wall[pl.ds(o * 4 + q, 1), :]
            send_w[pl.ds(slot, 1), :] = jnp.where(row_of_lane < live - q * ROWS, weight, 0.0)
            return c

        return lax.fori_loop(0, grains, one, c)

    lax.fori_loop(0, nblock, place, 0)


def pack(region, count, partner, pos, rinv, anom, innov):
    members = anom.shape[2]
    vmem, smem = pl.BlockSpec(memory_space=pltpu.VMEM), pl.BlockSpec(memory_space=pltpu.SMEM)
    hbm = pl.BlockSpec(memory_space=pl.ANY)
    return pl.pallas_call(
        pack_kernel,
        out_shape=(
            jax.ShapeDtypeStruct((SEND, ROWS, members + HALF), bf16),
            jax.ShapeDtypeStruct((SEND, ROWS, HALF), bf16),
            jax.ShapeDtypeStruct((SEND, 128), f32),
            jax.ShapeDtypeStruct((8, 128), i32),
        ),
        in_specs=[smem, smem, vmem, vmem, vmem, hbm, hbm],
        out_specs=(vmem, vmem, vmem, vmem),
        scratch_shapes=[
            pltpu.VMEM((128, 128), f32),
            pltpu.VMEM((2, *anom.shape), bf16),
            *[pltpu.SMEM((NR,), i32)] * 5,
            pltpu.SemaphoreType.DMA((2,)),
        ],
        compiler_params=pltpu.CompilerParams(vmem_limit_bytes=16 * MIB),
    )(region, count, partner, pos, rinv, anom, innov)


def exchange_kernel(send, send_b, send_w, head, total, flag_out, *scratch):
    scratch = list(scratch)

    def take(n):
        out = scratch[:n]
        del scratch[:n]
        return out

    zm, zs, bm, bs = take(LISTS), take(LISTS + 1), take(LISTS), take(LISTS + 1)
    wm, ws = take(LISTS), take(LISTS + 1)
    hm, hs, hsm, pn, pw, kept_a, kept_w, acc, ff = take(9)
    p, ro, rd, sb, u, ro2, rd2, sb2 = (take(2) for _ in range(8))
    zsend, zrecv, ssend, srecv, hsem, sems, recvs, fsend, frecv = take(9)

    members = acc.shape[3]
    x, tile = lax.axis_index("grp"), lax.axis_index("tile")
    z, inner = tile // 8, tile % 8
    y, core = inner // 2, inner % 2
    sibling = tile + 1 - 2 * core

    def around(step):
        return x, lax.rem(z + step, NZ) * 8 + inner

    def along(axis, step):
        if axis == 0:
            return x, z * 8 + lax.rem(y + step, NY) * 2 + core
        return lax.rem(x + step, NX), tile

    ways = (around(1), around(NZ - 1))
    barrier = pltpu.get_barrier_semaphore()
    for other in (*ways, (x, sibling), along(0, 1), along(0, 3), along(1, 1), along(1, 3)):
        pl.semaphore_signal(barrier, inc=1, device_id=other, device_id_type=MESH)
    pl.semaphore_wait(barrier, 7)

    def copy(src, dst, send_sem, recv_sem, other):
        return pltpu.make_async_remote_copy(
            src_ref=src, dst_ref=dst, send_sem=send_sem, recv_sem=recv_sem, device_id=other, device_id_type=MESH
        )

    edges = (0, *CAPS[::-1])

    def hop_copies(way, hop):
        entry = way * HOPS + hop
        base = way * CAPS[0]
        out = []
        for k in range(HOPS - hop):
            lo, n = edges[k], edges[k + 1] - edges[k]
            src = send.at[pl.ds(base + lo, n)] if hop == 0 else zm[entry - 1].at[pl.ds(lo, n)]
            out.append((k, src, zm[entry].at[pl.ds(lo, n)]))
        rows = WCAPS[hop]
        out.append((4, send_w.at[pl.ds(base, rows)] if hop == 0 else wm[entry - 1].at[pl.ds(0, rows)], wm[entry]))
        out.append((5, head if hop == 0 else hm.at[entry - 1], hm.at[entry]))
        for k in range(HOPS - hop):
            lo, n = edges[k], edges[k + 1] - edges[k]
            src = send_b.at[pl.ds(base + lo, n)] if hop == 0 else bm[entry - 1].at[pl.ds(lo, n)]
            out.append((6 + k, src, bm[entry].at[pl.ds(lo, n)]))
        return {k: copy(src, dst, zsend.at[way, hop, k], zrecv.at[way, hop, k], ways[way]) for k, src, dst in out}

    z_copies = [[hop_copies(way, hop) for hop in range(HOPS)] for way in range(2)]
    order = [[5, 4, *range(HOPS - hop)] for hop in range(HOPS)]
    stay = pl.ds(2 * CAPS[0], STAY)
    pairs = [((hm.at[e], hs.at[e]), (zm[e], zs[e]), (wm[e], ws[e]), (bm[e], bs[e])) for e in range(LISTS)]
    pairs.append((
        (head, hs.at[LISTS]), (send.at[stay], zs[LISTS]), (send_w.at[stay], ws[LISTS]), (send_b.at[stay], bs[LISTS])
    ))
    side = [
        [copy(s, t, ssend.at[e, i], srecv.at[e, i], (x, sibling)) for i, (s, t) in enumerate(pairs[e])] for e in range(LISTS + 1)
    ]
    to_scalar = [pltpu.make_async_copy(hm.at[e], hsm.at[e], hsem.at[e]) for e in range(LISTS)]
    to_scalar.append(pltpu.make_async_copy(head, hsm.at[LISTS], hsem.at[LISTS]))
    to_scalar += [pltpu.make_async_copy(hs.at[e], hsm.at[LISTS + 1 + e], hsem.at[LISTS + 1 + e]) for e in range(LISTS + 1)]

    for k in order[0]:
        for way in range(2):
            z_copies[way][0][k].start()
    for c in side[LISTS]:
        c.start()
    to_scalar[LISTS].start()

    expand = (lax.broadcasted_iota(i32, (1024, 64), 0) // 16 == lax.broadcasted_iota(i32, (1024, 64), 1)).astype(bf16)
    keep = (lax.broadcasted_iota(i32, (1024, 128), 0) % 16 == lax.broadcasted_iota(i32, (1024, 128), 1) % 16).astype(f32)
    pick = (lax.broadcasted_iota(i32, (8, 128), 1) // 16 == lax.broadcasted_iota(i32, (8, 128), 0)).astype(bf16)

    own_stage, far_stage = (LISTS,), (HOPS - 1, LISTS - 1)
    stages = [own_stage, *((way * HOPS + hop,) for hop in range(HOPS - 1) for way in range(2)), far_stage]

    def place_of(at, entry, r):
        row, shift = (1, 0) if entry == LISTS else (0, entry // HOPS * NR)
        value = hsm[at, row, shift + r]
        return value // 256, value % 256

    def slots(entries, who, r):
        found = []
        for entry in entries:
            start, grains = place_of(entry + who * (LISTS + 1), entry, r)
            own = entry == LISTS
            base = 2 * CAPS[0] if own and not who else 0
            cap = STAY if own else CAPS[entry % HOPS]
            found.append((start, grains, base, cap))
        out = []
        for i in range(8):
            start, grains, base, cap = found[0]
            slot = base + jnp.minimum(start + i, cap - 1)
            if len(found) == 1:
                out.append((None, slot, None, i < grains))
            else:
                start_2, grains_2, _, cap_2 = found[1]
                slot_2 = jnp.clip(start_2 + i - grains, 0, cap_2 - 1)
                out.append((i < grains, slot, slot_2, i < grains + grains_2))
        return out

    def sources(entries, who, mine, theirs, own):
        return [theirs[e] if who else (own if e == LISTS else mine[e]) for e in entries]

    def multiply(stage, target):
        for yp in range(NY):
            turned = pn[yp].astype(f32).T
            anomalies = kept_a[stage, yp]
            for b in range(8):
                weight = kept_w[stage, b : b + 1, yp * 256 : (yp + 1) * 256]
                product = jnp.dot((turned * weight).astype(bf16), anomalies, preferred_element_type=f32)
                if stage == 0:
                    acc[yp, b] = product
                elif stage < STAGES - 1:
                    acc[yp, b] += product
                elif b % 2 == 0:
                    target[0, yp, b // 2] = (acc[yp, b] + product).astype(bf16)
                else:
                    target[1, b // 2, yp] = (acc[yp, b] + product).astype(bf16)

    def first_columns(stage):
        entries = stages[stage]

        def gather(yp, carry):
            r = z * 8 + yp * 2 + core
            for who in range(2):
                panels = sources(entries, who, zm, zs, send)
                weights = sources(entries, who, wm, ws, send_w)
                for i, (first_list, slot, slot_2, live) in enumerate(slots(entries, who, r)):
                    panel, weight = panels[0][slot], weights[0][pl.ds(slot, 1), :]
                    if first_list is not None:
                        panel = jnp.where(first_list, panel, panels[1][slot_2])
                        weight = jnp.where(first_list, weight, weights[1][pl.ds(slot_2, 1), :])
                    rows = pl.ds(who * 128 + i * ROWS, ROWS)
                    kept_a[stage, yp, rows, :] = panel[:, 0:members]
                    pn[yp, rows, :] = panel[:, members : members + HALF]
                    pw[pl.ds(yp * 16 + who * 8 + i, 1), :] = jnp.where(live, weight, 0.0)
            return carry

        lax.fori_loop(0, NY, gather, 0)
        wide = jnp.dot(expand, pw[...].astype(bf16), preferred_element_type=f32) * keep
        kept_w[stage] = lax.dot_general(pick, wide.astype(bf16), (((1,), (1,)), ((), ())), preferred_element_type=f32)
        multiply(stage, p[0])

    def other_columns(stage):
        entries = stages[stage]

        def gather(yp, carry):
            r = z * 8 + yp * 2 + core
            for who in range(2):
                panels = sources(entries, who, bm, bs, send_b)
                for i, (first_list, slot, slot_2, live) in enumerate(slots(entries, who, r)):
                    panel = panels[0][slot]
                    if first_list is not None:
                        panel = jnp.where(first_list, panel, panels[1][slot_2])
                    pn[yp, pl.ds(who * 128 + i * ROWS, ROWS), :] = panel
            return carry

        lax.fori_loop(0, NY, gather, 0)
        multiply(stage, p[1])

    def ready(entry):
        for c in side[entry][0:3]:
            c.wait_recv()
        for at in (entry, LISTS + 1 + entry):
            if at > LISTS:
                to_scalar[at].start()
            to_scalar[at].wait()

    def wide_of(ref):
        return ref[...].astype(f32)

    def flag_copy(src, dst, k, axis, step):
        return copy(ff.at[src], ff.at[dst], fsend.at[k], frecv.at[k], along(axis, step))

    flags = [
        flag_copy(0, 1, 0, 0, 1), flag_copy(0, 2, 1, 0, 3), flag_copy(3, 4, 2, 0, 1),
        flag_copy(5, 6, 3, 1, 1), flag_copy(5, 7, 4, 1, 3), flag_copy(8, 9, 5, 1, 1),
    ]

    def reducer(part):
        p_, ro_, rd_, sb_, u_, ro2_, rd2_, sb2_ = (buffers[part] for buffers in (p, ro, rd, sb, u, ro2, rd2, sb2))
        rows = HALF // 2

        def half_copy(src, dst, half, phase, k, axis, step):
            return copy(src, dst, sems.at[part, half, phase, k], recvs.at[part, half, phase, k], along(axis, step))

        def triple(me):
            return lax.rem(me + 1, 4), lax.rem(me + 3, 4), lax.rem(me + 2, 4)

        first, second = [], []
        for half in range(2):
            me, other = (y, x) if half == 0 else (x, y)
            right, left, far = triple(me)
            lo, hi = pl.ds(0, 2), pl.ds(2, 2)
            first.append([
                half_copy(p_.at[half, far, lo], ro_.at[half, 0], half, 0, 0, half, 1),
                half_copy(p_.at[half, far, hi], ro_.at[half, 1], half, 0, 1, half, 3),
                half_copy(p_.at[half, right, hi], rd_.at[half, 0, hi], half, 0, 2, half, 1),
                half_copy(p_.at[half, left, lo], rd_.at[half, 1, lo], half, 0, 3, half, 3),
                half_copy(sb_.at[half, 0], rd_.at[half, 0, lo], half, 0, 4, half, 1),
                half_copy(sb_.at[half, 1], rd_.at[half, 1, hi], half, 0, 5, half, 3),
            ])
            axis = 1 - half
            right, left, far = triple(other)
            lo, hi = pl.ds(0, rows), pl.ds(rows, rows)
            second.append([
                half_copy(u_.at[half, far, lo], ro2_.at[half, 0], half, 1, 0, axis, 1),
                half_copy(u_.at[half, far, hi], ro2_.at[half, 1], half, 1, 1, axis, 3),
                half_copy(u_.at[half, right, hi], rd2_.at[half, 0, hi], half, 1, 2, axis, 1),
                half_copy(u_.at[half, left, lo], rd2_.at[half, 1, lo], half, 1, 3, axis, 3),
                half_copy(sb2_.at[half, 0], rd2_.at[half, 0, lo], half, 1, 4, axis, 1),
                half_copy(sb2_.at[half, 1], rd2_.at[half, 1, hi], half, 1, 5, axis, 3),
            ])

        def begin():
            for k in range(4):
                for half in range(2):
                    first[half][k].start()
            if part == 0:
                flag = head[...] + hs[LISTS]
                for e in range(LISTS):
                    flag = flag + hm[e] + hs[e]
                ff[0] = flag.astype(f32)
                flags[0].start()
                flags[1].start()

        def pass_on():
            for k in range(2):
                for half in range(2):
                    me = y if half == 0 else x
                    to = lax.rem(me + (1 if k == 0 else 3), 4)
                    first[half][k].wait_recv()
                    for i in range(2):
                        sb_[half, k, i] = (wide_of(p_.at[half, to, 2 * k + i]) + wide_of(ro_.at[half, k, i])).astype(bf16)
                    first[half][4 + k].start()
            if part == 0:
                flags[0].wait_recv()
                ff[3] = ff[0] + ff[1]
                flags[2].start()

        def turn():
            for half in range(2):
                me = y if half == 0 else x
                for k in (2, 3, 4, 5):
                    first[half][k].wait_recv()
                for i in range(4):
                    u_[half, i] = (
                        wide_of(p_.at[half, me, i]) + wide_of(rd_.at[half, 0, i]) + wide_of(rd_.at[half, 1, i])
                    ).astype(bf16)
                for k in range(4):
                    second[half][k].start()
            if part == 0:
                flags[1].wait_recv()
                flags[2].wait_recv()
                ff[5] = ff[0] + ff[2] + ff[4]
                flags[3].start()
                flags[4].start()

        def pass_on_again():
            for half in range(2):
                other = x if half == 0 else y
                for k in range(2):
                    to = lax.rem(other + (1 if k == 0 else 3), 4)
                    second[half][k].wait_recv()
                    sb2_[half, k] = (wide_of(u_.at[half, to, pl.ds(k * rows, rows)]) + wide_of(ro2_.at[half, k])).astype(bf16)
                    second[half][4 + k].start()
            if part == 0:
                flags[3].wait_recv()
                ff[8] = ff[5] + ff[6]
                flags[5].start()

        def finish():
            for half in range(2):
                other = x if half == 0 else y
                for k in (2, 3, 4, 5):
                    second[half][k].wait_recv()
                turned = wide_of(u_.at[half, other]) + wide_of(rd2_.at[half, 0]) + wide_of(rd2_.at[half, 1])
                total[half, :, part * HALF : (part + 1) * HALF] = turned.T
            if part == 0:
                flags[4].wait_recv()
                flags[5].wait_recv()
                flag_out[...] = ff[5] + ff[7] + ff[9]

        def drain():
            for c in (*first[0], *first[1], *second[0], *second[1]):
                c.wait_send()

        return begin, (pass_on, turn, pass_on_again, finish), drain

    begin_a, steps_a, drain_a = reducer(0)
    begin_b, steps_b, drain_b = reducer(1)

    for hop in range(HOPS):
        for k in order[hop]:
            for way in range(2):
                entry = way * HOPS + hop
                z_copies[way][hop][k].wait_recv()
                if hop + 1 < HOPS and k in z_copies[way][hop + 1]:
                    z_copies[way][hop + 1][k].start()
                if k == 5:
                    side[entry][0].start()
                    to_scalar[entry].start()
        for way in range(2):
            entry = way * HOPS + hop
            side[entry][1].start()
            side[entry][2].start()
        if hop == HOPS - 2:
            for k in range(HOPS):
                for way in range(2):
                    z_copies[way][0][6 + k].start()
        if hop == 0:
            ready(LISTS)
            first_columns(0)
        else:
            for way in range(2):
                ready(way * HOPS + hop - 1)
                first_columns(1 + 2 * (hop - 1) + way)
    for entry in far_stage:
        ready(entry)
    first_columns(STAGES - 1)
    begin_a()

    for hop in range(HOPS):
        for k in range(HOPS - hop):
            for way in range(2):
                z_copies[way][hop][6 + k].wait_recv()
                if hop + 1 < HOPS and 6 + k in z_copies[way][hop + 1]:
                    z_copies[way][hop + 1][6 + k].start()
        for way in range(2):
            side[way * HOPS + hop][3].start()
        if hop == 0:
            side[LISTS][3].wait_recv()
            other_columns(0)
            steps_a[0]()
        else:
            for way in range(2):
                side[way * HOPS + hop - 1][3].wait_recv()
                other_columns(1 + 2 * (hop - 1) + way)
                if way == 0:
                    steps_a[hop]()
    for entry in far_stage:
        side[entry][3].wait_recv()
    other_columns(STAGES - 1)
    begin_b()
    for step in steps_b:
        step()

    drain_a()
    drain_b()
    for way in range(2):
        for hop in range(HOPS):
            for k in z_copies[way][hop]:
                z_copies[way][hop][k].wait_send()
    for group in side:
        for c in group:
            c.wait_send()
    for c in flags:
        c.wait_send()


def exchange(send, send_b, send_w, head):
    vmem = pl.BlockSpec(memory_space=pltpu.VMEM)
    members = send.shape[2] - HALF
    square, slab, thin = (members, members), (HALF, members), (HALF // 2, members)
    dma = pltpu.SemaphoreType.DMA
    panels = [pltpu.VMEM((cap, ROWS, members + HALF), bf16) for cap in CAPS] * 2
    others = [pltpu.VMEM((cap, ROWS, HALF), bf16) for cap in CAPS] * 2
    weights = [pltpu.VMEM((cap, 128), f32) for cap in WCAPS] * 2
    return pl.pallas_call(
        exchange_kernel,
        out_shape=(
            jax.ShapeDtypeStruct((2, *square), f32),
            jax.ShapeDtypeStruct((8, 128), f32),
        ),
        in_specs=[vmem] * 4,
        out_specs=(vmem, vmem),
        scratch_shapes=[
            *panels,
            *panels,
            pltpu.VMEM((STAY, ROWS, members + HALF), bf16),
            *others,
            *others,
            pltpu.VMEM((STAY, ROWS, HALF), bf16),
            *weights,
            *weights,
            pltpu.VMEM((STAY, 128), f32),
            pltpu.VMEM((LISTS, 8, 128), i32),
            pltpu.VMEM((LISTS + 1, 8, 128), i32),
            pltpu.SMEM((2 * LISTS + 2, 8, 128), i32),
            pltpu.VMEM((NY, 256, HALF), bf16),
            pltpu.VMEM((NY * 16, 128), f32),
            pltpu.VMEM((STAGES, NY, 256, members), bf16),
            pltpu.VMEM((STAGES, 8, NY * 256), f32),
            pltpu.VMEM((NY, 8, *slab), f32),
            pltpu.VMEM((10, 8, 128), f32),
            *[pltpu.VMEM((2, 4, 4, *slab), bf16)] * 2,
            *[pltpu.VMEM((2, 2, 2, *slab), bf16)] * 2,
            *[pltpu.VMEM((2, 2, 4, *slab), bf16)] * 2,
            *[pltpu.VMEM((2, 2, 2, *slab), bf16)] * 2,
            *[pltpu.VMEM((2, 4, *slab), bf16)] * 2,
            *[pltpu.VMEM((2, 2, *thin), bf16)] * 2,
            *[pltpu.VMEM((2, 2, *slab), bf16)] * 2,
            *[pltpu.VMEM((2, 2, *thin), bf16)] * 2,
            dma((2, HOPS, 6 + HOPS)),
            dma((2, HOPS, 6 + HOPS)),
            dma((LISTS + 1, 4)),
            dma((LISTS + 1, 4)),
            dma((2 * LISTS + 2,)),
            dma((2, 2, 2, 6)),
            dma((2, 2, 2, 6)),
            dma((6,)),
            dma((6,)),
        ],
        compiler_params=pltpu.CompilerParams(collective_id=0, has_side_effects=True, vmem_limit_bytes=46 * MIB),
    )(send, send_b, send_w, head)


def update_kernel(state, coeff, total, updated, new_coeff, coef):
    @pl.when(pl.program_id(1) == 0)
    def _():
        new = (1.0 - relaxation) * coeff[...] + relaxation * total[...]
        new_coeff[...] = new
        coef[...] = new.astype(bf16)

    s = state[...]
    updated[...] = (s.astype(f32) + jnp.dot(s, coef[...], preferred_element_type=f32)).astype(bf16)


def update(state, coeff, total):
    _, blocks, width, members = state.shape
    step = 2048
    square = (members, members)
    rows = pl.BlockSpec((None, None, step, members), lambda j, i: (0, j, i, 0))
    one = pl.BlockSpec((None, None, *square), lambda j, i: (0, j, 0, 0))
    return pl.pallas_call(
        update_kernel,
        grid=(blocks, width // step),
        out_shape=(jax.ShapeDtypeStruct(state.shape, bf16), jax.ShapeDtypeStruct(coeff.shape, f32)),
        in_specs=[rows, one, pl.BlockSpec((None, *square), lambda j, i: (j, 0, 0))],
        out_specs=(rows, one),
        scratch_shapes=[pltpu.VMEM(square, bf16)],
        compiler_params=pltpu.CompilerParams(vmem_limit_bytes=16 * MIB),
    )(state, coeff, total)


def padded_total(obs_anom, innov, obs_rinv, obs_pos, obs_count, obs_region, obs_partner, blocks, width):
    tile_count = lax.axis_size("tile")
    nblock, observation_count, ensemble_members = obs_anom.shape
    partition_count = obs_partner.shape[1]
    nlocal = lax.axis_size("grp") * blocks
    per_neighbour = max(2, (2 * nblock + tile_count - 1) // tile_count)
    slot_count = tile_count * per_neighbour
    slot_grouping = 8
    region = obs_region[:, 0]
    order = jnp.arange(nblock, dtype=jnp.int32)
    before = (region[None, :] == region[:, None]) & (order[None, :] < order[:, None])
    destination = region * per_neighbour + jnp.sum(before.astype(jnp.int32), axis=1)
    assignment_rule = destination[None, :] == jnp.arange(slot_count, dtype=jnp.int32)[:, None]
    place_half = assignment_rule.astype(jnp.bfloat16)
    place_int = assignment_rule.astype(jnp.int32)
    labels = jnp.concatenate([obs_count[:, None], obs_partner], axis=1)
    sent_labels = jnp.dot(place_int, labels).reshape(tile_count, per_neighbour, partition_count + 1)
    stacked = jnp.concatenate([obs_anom, innov], axis=2).reshape(nblock, -1)
    packed = jnp.dot(place_half, stacked, preferred_element_type=jnp.bfloat16)
    packed = packed.reshape(tile_count, per_neighbour, observation_count, 2 * ensemble_members)
    sent_pos = jnp.dot(place_int, obs_pos).reshape(tile_count, per_neighbour, observation_count)
    sent_var = jnp.dot(assignment_rule.astype(jnp.float32), obs_rinv, precision=lax.Precision.HIGHEST)
    sent_var = sent_var.reshape(tile_count, per_neighbour, observation_count)

    def exchange(array):
        return lax.all_to_all(array, "tile", split_axis=0, concat_axis=0, tiled=True)

    received_panels = exchange(packed).reshape(slot_count, observation_count, 2 * ensemble_members)
    flattened_labels = exchange(sent_labels).reshape(slot_count, partition_count + 1)
    recv_anom = received_panels[:, :, :ensemble_members]
    recv_innov = received_panels[:, :, ensemble_members:]
    flattened_positions = exchange(sent_pos).reshape(slot_count, observation_count)
    flattened_variances = exchange(sent_var).reshape(slot_count, observation_count)
    partners = flattened_labels[:, 1:]
    block_index = jnp.arange(nlocal, dtype=jnp.int32)

    def accumulate_group(step, total):
        start = step * slot_grouping

        def part(array):
            return lax.dynamic_slice_in_dim(array, start, slot_grouping, 0)

        weights = taper_weights(
            part(flattened_positions), part(partners), part(flattened_labels)[:, 0], part(flattened_variances), width,
            ensemble_members,
        )
        scaled_part = (weights[..., None] * part(recv_innov)[:, None].astype(jnp.float32)).astype(jnp.bfloat16)
        picked = (part(partners)[..., None] == block_index).astype(jnp.bfloat16)
        by_block = jnp.einsum("qkb,qkin->qbin", picked, scaled_part, preferred_element_type=jnp.float32).astype(jnp.bfloat16)
        return total + jnp.einsum("qim,qbin->bmn", part(recv_anom), by_block, preferred_element_type=jnp.float32)

    initial_total = jnp.zeros((nlocal, ensemble_members, ensemble_members), jnp.float32)
    running_totals = lax.fori_loop(0, slot_count // slot_grouping, accumulate_group, initial_total)
    return lax.psum_scatter(running_totals.astype(jnp.bfloat16), "grp", scatter_dimension=0, tiled=True).astype(jnp.float32)


def on_device(obs_anom, innov, obs_rinv, obs_pos, obs_count, obs_region, obs_partner, state_anom, coeff):
    send, send_b, send_w, head = pack(obs_region[:, 0], obs_count, obs_partner.T, obs_pos, obs_rinv, obs_anom, innov)
    fast, flags = exchange(send, send_b, send_w, head)
    blocks, width = state_anom.shape[1:3]
    total = lax.cond(
        flags[1, NR] > 0,
        lambda *obs: padded_total(*obs[:-1], blocks, width),
        lambda *obs: obs[-1],
        obs_anom, innov, obs_rinv, obs_pos, obs_count, obs_region, obs_partner, fast,
    )
    return update(state_anom, coeff, total)


def solution(mesh):
    return jax.shard_map(
        on_device,
        mesh=mesh,
        in_specs=(
            P(("grp", "tile"), None, None),
            P(("grp", "tile"), None, None),
            P(("grp", "tile"), None),
            P(("grp", "tile"), None),
            P(("grp", "tile")),
            P(("grp", "tile"), None),
            P(("grp", "tile"), None),
            P("grp", "tile", None, None),
            P("grp", "tile", None, None),
        ),
        out_specs=(P("grp", "tile", None, None), P("grp", "tile", None, None)),
        check_vma=False,
    )
```

time: 150 us -> 137 us (0.913)
  Pallas kernels: 132 us -> 118 us
    pallas_call x1, Pallas kernels: 121 us -> 109 us  [exchange(): pl.pallas_call(exchange_kernel, out_shape=(jax.ShapeDtypeStruct((2, *squa...]
where the time goes in v3:
time: 137 us
  Pallas kernels  118 us (86%)
  between operations  14.8 us (11%)
  local copies, waits for them, and re-layouts  3.81 us (3%)
    pallas_call x1, Pallas kernels, exchange(): pl.pallas_call(exchange_kernel, out_shape=(jax.ShapeDtypeStruct((2, *squa...  109 us
    pallas_call x1, Pallas kernels, pack(): pl.pallas_call(pack_kernel, out_shape=(jax.ShapeDtypeStruct((SEND, ROWS,...  5.56 us
    pallas_call x1, Pallas kernels, update(): pl.pallas_call(update_kernel, grid=(blocks, width // step), out_shape=(ja...  3.36 us
    unnamed x14, local copies, waits for them, and re-layouts  3.23 us

profile of v3, /device:TPU:8, one launch (start us, length us, event | category | flops | bytes accessed | tf_op | source)
XLA Modules:
  0.0 136.8 jit_solution(15626064382404422585)
XLA Ops:
  7.2 0.0 copy-start.2
  7.2 0.0 copy-start.3
  7.2 0.0 copy-start.4
  7.2 0.0 copy-start.5
  7.2 0.0 copy-start.6
  7.2 5.6 %shard_map.104 = (bf16[168,16,384]{2,1,0:T(8,128)(2,1)S(1)}, bf16[168,16,128]{2,1,0:T(8,128)(2,1)S(1)}, f32[168,128]{1,0:T(8,128)S(1)}, s32[8,128]{1,0:T(8,128)S(1)}) custom-call(s32[32]{0:T(128)} %bitcast.70, s32[32]{0:T(128)} %count.1, s32[6,32]{1,0:T(8,128)} %bitcast.67, s32[32,64]{1,0:T(8,128)} %pos.1, f32[32,64]{1,0:T(8,128)} %rinv.1, ...), custom_call_target="tpu_custom_call" | custom-call | tf_op jit(solution)/shard_map/pallas_call | solution.py:179
  12.8 109.2 %shard_map.105 = (f32[2,256,256]{2,1,0:T(8,128)S(1)}, f32[8,128]{1,0:T(8,128)S(1)}) custom-call(bf16[168,16,384]{2,1,0:T(8,128)(2,1)S(1)} %get-tuple-element.187.send, bf16[168,16,128]{2,1,0:T(8,128)(2,1)S(1)} %get-tuple-element.188.send_b, f32[168,128]{1,0:T(8,128)S(1)} %get-tuple-element.189.send_w, s32[8,128]{1,0:T(8,128)S(1)} %get-tuple-element.190.head), custom_call_target="tpu_custom_call" | custom-call | tf_op jit(solution)/shard_map/pallas_call | solution.py:578
  122.0 0.6 slice.19
  123.3 0.0 copy-done.2
  123.3 0.0 copy-done.3
  123.3 0.0 copy-done.4
  123.3 0.0 copy-done.5
  123.3 0.0 copy-done.6
  123.3 0.0 copy-start.1
  123.4 1.0 copy-done.1
  124.4 0.0 copy-start
  124.4 2.2 %copy-done = bf16[1,2,4096,256]{3,2,1,0:T(8,128)(2,1)S(1)} copy-done((bf16[1,2,4096,256]{3,2,1,0:T(8,128)(2,1)S(1)}, bf16[1,2,4096,256]{3,2,1,0:T(8,128)(2,1)}, u32[]{:S(2)}) %copy-start) | copy-done | bytes 4194328
  126.6 3.4 %shard_map.106 = (bf16[1,2,4096,256]{3,2,1,0:T(8,128)(2,1)}, f32[1,2,256,256]{3,2,1,0:T(8,128)}) custom-call(bf16[1,2,4096,256]{3,2,1,0:T(8,128)(2,1)S(1)} %copy-done, f32[1,2,256,256]{3,2,1,0:T(8,128)S(1)} %copy-done.1, f32[2,256,256]{2,1,0:T(8,128)S(1)} %get-tuple-element.246.total), custom_call_target="tpu_custom_call" | custom-call | tf_op jit(solution)/shard_map/pallas_call | solution.py:644
  (1 shorter events, 0.0 us)
Async XLA Ops:
  7.2 116.1 %copy-start.2 = (s32[32,64]{1,0:T(8,128)S(1)}, s32[32,64]{1,0:T(8,128)}, u32[]{:S(2)}) copy-start(s32[32,64]{1,0:T(8,128)} %pos.1) | copy-start | bytes 24580
  7.2 116.1 %copy-start.3 = (f32[32,64]{1,0:T(8,128)S(1)}, f32[32,64]{1,0:T(8,128)}, u32[]{:S(2)}) copy-start(f32[32,64]{1,0:T(8,128)} %rinv.1) | copy-start | bytes 24580
  7.2 116.1 %copy-start.4 = (s32[32,6]{0,1:T(8,128)S(1)}, s32[32,6]{0,1:T(8,128)}, u32[]{:S(2)}) copy-start(s32[32,6]{0,1:T(8,128)} %param.19) | copy-start | bytes 2308
  7.2 116.1 %copy-start.5 = (s32[32]{0:T(128)S(1)}, s32[32]{0:T(128)}, u32[]{:S(2)}) copy-start(s32[32]{0:T(128)} %count.1) | copy-start | bytes 388
  7.2 116.1 %copy-start.6 = (s32[32,1]{0,1:T(1,128)S(1)}, s32[32,1]{0,1:T(1,128)}, u32[]{:S(2)}) copy-start(s32[32,1]{0,1:T(1,128)} %param.18) | copy-start | bytes 388
  123.3 1.0 copy-start.1
  124.4 2.2 %copy-start = (bf16[1,2,4096,256]{3,2,1,0:T(8,128)(2,1)S(1)}, bf16[1,2,4096,256]{3,2,1,0:T(8,128)(2,1)}, u32[]{:S(2)}) copy-start(bf16[1,2,4096,256]{3,2,1,0:T(8,128)(2,1)} %state.1) | copy-start | bytes 12582916

commit v4 on v3

--- a/solution.py
+++ b/solution.py
@@ -11,9 +11,10 @@
 MIB = 1024 * 1024
 
 ROWS = 16
-CAPS = (64, 50, 40, 28)
-STAY = 40
+CAPS = (56, 46, 34, 24)
+STAY = 32
 SEND = 2 * CAPS[0] + STAY
+SPARE = 8
 HOPS = len(CAPS)
 NZ, NY, NX, NR = 8, 4, 4, 64
 LISTS = 2 * HOPS
@@ -31,7 +32,9 @@
     return jnp.where(live[..., None, :], weight, 0.0)
 
 
-def pack_kernel(region, count, partner, pos, rinv, anom, innov, send, send_b, send_w, head, wall, held, size, fill, first, seat_a, seat_b, sem):
+def pack_kernel(
+    region, count, partner, pos, rinv, anom, innov, send, send_b, send_w, head, wall, held, size, fill, seats, place_at, sem
+):
     nblock, members = anom.shape[0], anom.shape[2]
     width = 4096.0
     z = lax.axis_index("tile") // 8
@@ -39,10 +42,11 @@
     for c in loads:
         c.start()
 
-    lane = lax.broadcasted_iota(i32, (128, 128), 1)
-    repeat = (lax.broadcasted_iota(i32, (128, nblock), 0) // 4 == lax.broadcasted_iota(i32, (128, nblock), 1)).astype(f32)
-    column = lax.broadcasted_iota(i32, (128, 64), 1)
-    quarter = (column // 16 == lax.broadcasted_iota(i32, (128, 64), 0) % 4).astype(f32)
+    deep = 8 * nblock
+    lane = lax.broadcasted_iota(i32, (deep, 128), 1)
+    repeat = (lax.broadcasted_iota(i32, (deep, nblock), 0) // 8 == lax.broadcasted_iota(i32, (deep, nblock), 1)).astype(f32)
+    column = lax.broadcasted_iota(i32, (deep, 64), 1)
+    quarter = (column // 16 == lax.broadcasted_iota(i32, (deep, 64), 0) % 8).astype(f32)
     fold = (lax.broadcasted_iota(i32, (64, 128), 0) % 16 == lax.broadcasted_iota(i32, (64, 128), 1) % 16).astype(f32)
 
     def exact(a, b):
@@ -55,7 +59,7 @@
         repeat, partner[...].astype(f32), (((1,), (1,)), ((), ())), precision=lax.Precision.HIGHEST, preferred_element_type=f32
     )
     block_of_lane = (lane // 16).astype(f32)
-    paired = jnp.zeros((128, 128), f32)
+    paired = jnp.zeros((deep, 128), f32)
     for k in range(partner.shape[0]):
         paired = jnp.where(partners[:, k : k + 1] == block_of_lane, 1.0, paired)
     center = (block_of_lane + 0.5) * width
@@ -67,22 +71,22 @@
         fill[i] = 0
         return c
 
-    lax.fori_loop(0, NR, clear, 0)
+    lax.fori_loop(0, NR, clear, 0, unroll=16)
 
     def blank(i, c):
         send[i] = jnp.zeros(send.shape[1:], bf16)
         send_b[i] = jnp.zeros(send_b.shape[1:], bf16)
         return c
 
-    lax.fori_loop(0, SEND, blank, 0)
+    lax.fori_loop(0, SEND + SPARE, blank, 0, unroll=8)
     send_w[...] = jnp.zeros_like(send_w)
 
     def measure(o, c):
         r = region[o]
-        size[r] = size[r] + (count[o] + 15) // 16
+        size[r] = size[r] + count[o]
         return c
 
-    lax.fori_loop(0, nblock, measure, 0)
+    lax.fori_loop(0, nblock, measure, 0, unroll=8)
 
     def plane(distance):
         return lax.rem(z + distance, NZ) * 8
@@ -91,85 +95,89 @@
         base = plane(distance)
         return sum(size[base + i] for i in range(8))
 
-    d = [total(distance) for distance in range(NZ)]
-    right, left = d[1] + d[2] + d[3], d[5] + d[6] + d[7]
-    far_right = jnp.clip((d[4] + left - right + 1) // 2, 0, d[4])
-    far_left = d[4] - far_right
-    counts = (
-        (right + far_right, d[2] + d[3] + far_right, d[3] + far_right, far_right),
-        (left + far_left, d[6] + d[5] + far_left, d[5] + far_left, far_left),
-    )
-    over = (d[0] > STAY).astype(i32)
-    for way in range(2):
-        for hop in range(HOPS):
-            over = over | (counts[way][hop] > CAPS[hop]).astype(i32)
-
     head_row = lax.broadcasted_iota(i32, (8, 128), 0)
     head_lane = lax.broadcasted_iota(i32, (8, 128), 1)
 
     def noted(header, row, at, value):
         return jnp.where((head_row == row) & (head_lane == at), value, header)
 
-    header = noted(jnp.zeros((8, 128), i32), 1, NR, over)
+    def begin(used, n):
+        return jnp.where(used % ROWS + n > 8 * ROWS, (used + ROWS - 1) // ROWS * ROWS, used)
 
     def seat_far(i, carry):
-        used_right, used_left, header = carry
+        used_right, used_left, load_right, load_left, header = carry
         r = plane(4) + i
         n = size[r]
-        a = jnp.minimum(n, far_right - used_right)
-        b = n - a
-        header = noted(noted(header, 0, r, used_right * 256 + a), 0, NR + r, used_left * 256 + b)
-        first[r] = a
-        seat_a[r] = used_right
-        seat_b[r] = CAPS[0] + used_left
-        return used_right + a, used_left + b, header
-
-    used_right, used_left, header = lax.fori_loop(0, 8, seat_far, (jnp.int32(0), jnp.int32(0), header))
+        to_right = load_right <= load_left
+        right, left = begin(used_right, n), begin(used_left, n)
+        header = noted(header, 0, r, jnp.where(to_right, right * 256 + n, 0))
+        header = noted(header, 0, NR + r, jnp.where(to_right, 0, left * 256 + n))
+        seats[r] = jnp.where(to_right, right, CAPS[0] * ROWS + left)
+        used_right, used_left = jnp.where(to_right, right + n, used_right), jnp.where(to_right, used_left, left + n)
+        load_right, load_left = jnp.where(to_right, load_right + n, load_right), jnp.where(to_right, load_left, load_left + n)
+        return used_right, used_left, load_right, load_left, header
+
+    loads_of = (total(1) + total(2) + total(3), total(5) + total(6) + total(7))
+    none = jnp.zeros((), i32)
+    used_right, used_left, _, _, header = lax.fori_loop(0, 8, seat_far, (none, none, *loads_of, jnp.zeros((8, 128), i32)), unroll=8)
 
     def seat_near(distance, base, row, shift, carry):
         def seat(i, carry):
             used, header = carry
             r = plane(distance) + i
             n = size[r]
-            first[r] = n
-            seat_a[r] = base + used
-            seat_b[r] = base + used
-            return used + n, noted(header, row, shift + r, used * 256 + n)
-
-        return lax.fori_loop(0, 8, seat, carry)
-
-    for distance in (3, 2, 1):
+            first = begin(used, n)
+            seats[r] = base * ROWS + first
+            return first + n, noted(header, row, shift + r, first * 256 + n)
+
+        return lax.fori_loop(0, 8, seat, carry, unroll=8)
+
+    over = (used_right > CAPS[3] * ROWS) | (used_left > CAPS[3] * ROWS)
+    for hop, distance in ((2, 3), (1, 2), (0, 1)):
         used_right, header = seat_near(distance, 0, 0, 0, (used_right, header))
-    for distance in (5, 6, 7):
-        used_left, header = seat_near(distance, CAPS[0], 0, NR, (used_left, header))
-    _, header = seat_near(0, 2 * CAPS[0], 1, 0, (jnp.int32(0), header))
-    head[...] = header
+        used_left, header = seat_near(NZ - distance, CAPS[0], 0, NR, (used_left, header))
+        over = over | (used_right > CAPS[hop] * ROWS) | (used_left > CAPS[hop] * ROWS)
+    used_stay, header = seat_near(0, 2 * CAPS[0], 1, 0, (none, header))
+    over = over | (used_stay > STAY * ROWS)
+    head[...] = noted(header, 1, NR, over.astype(i32))
+
+    def find(o, c):
+        r = region[o]
+        place_at[o] = seats[r] + fill[r]
+        fill[r] = fill[r] + count[o]
+        return c
+
+    lax.fori_loop(0, nblock, find, 0, unroll=8)
     for c in loads:
         c.wait()
 
-    row_of_lane = lax.broadcasted_iota(i32, (1, 128), 1) % 16
+    deep_window = 5 * ROWS
+    to_row = lax.broadcasted_iota(i32, (deep_window, 64), 0)
+    from_row = lax.broadcasted_iota(i32, (deep_window, 64), 1)
+
+    sub = lax.broadcasted_iota(i32, (8, 128), 0)
+    row_of_lane = lax.broadcasted_iota(i32, (8, 128), 1) % ROWS
 
     def place(o, c):
-        r, live = region[o], count[o]
-        grains = (live + 15) // 16
-        start = fill[r]
-        fill[r] = start + grains
-        a, b, most = seat_a[r], seat_b[r], first[r]
-
-        def one(q, c):
-            f = start + q
-            slot = jnp.minimum(jnp.where(f < most, a + f, b + f - most), SEND - 1)
-            rows = pl.ds(pl.multiple_of(q * ROWS, ROWS), ROWS)
-            send[slot, :, 0:members] = held[0, o, rows, :]
-            send[slot, :, members : members + HALF] = held[1, o, rows, 0:HALF]
-            send_b[slot] = held[1, o, rows, HALF:members]
-            weight = wall[pl.ds(o * 4 + q, 1), :]
-            send_w[pl.ds(slot, 1), :] = jnp.where(row_of_lane < live - q * ROWS, weight, 0.0)
-            return c
-
-        return lax.fori_loop(0, grains, one, c)
-
-    lax.fori_loop(0, nblock, place, 0)
+        live, at = count[o], place_at[o]
+        shift = at % ROWS
+        grain = jnp.minimum(at // ROWS, SEND + SPARE - 8)
+        weight = jnp.where(sub * ROWS + row_of_lane < live, wall[pl.ds(pl.multiple_of(o * 8, 8), 8), :], 0.0)
+        same = pltpu.roll(weight, shift, 1)
+        next_one = pltpu.roll(pltpu.roll(weight, 1, 0), shift + 128 - ROWS, 1)
+        send_w[pl.ds(grain, 8), :] += jnp.where(row_of_lane >= shift, same, next_one)
+
+        move = ((to_row - shift == from_row) & (from_row < live)).astype(bf16)
+        anomalies = jnp.dot(move, held[0, o], preferred_element_type=f32).astype(bf16)
+        innovations = jnp.dot(move, held[1, o], preferred_element_type=f32).astype(bf16)
+        for q in range(5):
+            rows = slice(q * ROWS, (q + 1) * ROWS)
+            send[grain + q, :, 0:members] += anomalies[rows]
+            send[grain + q, :, members : members + HALF] += innovations[rows, 0:HALF]
+            send_b[grain + q] += innovations[rows, HALF:members]
+        return c
+
+    lax.fori_loop(0, nblock, place, 0, unroll=8)
 
 
 def pack(region, count, partner, pos, rinv, anom, innov):
@@ -179,17 +187,18 @@
     return pl.pallas_call(
         pack_kernel,
         out_shape=(
-            jax.ShapeDtypeStruct((SEND, ROWS, members + HALF), bf16),
-            jax.ShapeDtypeStruct((SEND, ROWS, HALF), bf16),
-            jax.ShapeDtypeStruct((SEND, 128), f32),
+            jax.ShapeDtypeStruct((SEND + SPARE, ROWS, members + HALF), bf16),
+            jax.ShapeDtypeStruct((SEND + SPARE, ROWS, HALF), bf16),
+            jax.ShapeDtypeStruct((SEND + SPARE, 128), f32),
             jax.ShapeDtypeStruct((8, 128), i32),
         ),
         in_specs=[smem, smem, vmem, vmem, vmem, hbm, hbm],
         out_specs=(vmem, vmem, vmem, vmem),
         scratch_shapes=[
-            pltpu.VMEM((128, 128), f32),
+            pltpu.VMEM((8 * anom.shape[0], 128), f32),
             pltpu.VMEM((2, *anom.shape), bf16),
-            *[pltpu.SMEM((NR,), i32)] * 5,
+            *[pltpu.SMEM((NR,), i32)] * 3,
+            pltpu.SMEM((anom.shape[0],), i32),
             pltpu.SemaphoreType.DMA((2,)),
         ],
         compiler_params=pltpu.CompilerParams(vmem_limit_bytes=16 * MIB),
@@ -207,7 +216,7 @@
     zm, zs, bm, bs = take(LISTS), take(LISTS + 1), take(LISTS), take(LISTS + 1)
     wm, ws = take(LISTS), take(LISTS + 1)
     hm, hs, hsm, pn, pw, kept_a, kept_w, acc, ff = take(9)
-    p, ro, rd, sb, u, ro2, rd2, sb2 = (take(2) for _ in range(8))
+    p, ro, rd, sb, u, rd2 = (take(2) for _ in range(6))
     zsend, zrecv, ssend, srecv, hsem, sems, recvs, fsend, frecv = take(9)
 
     members = acc.shape[3]
@@ -226,9 +235,9 @@
 
     ways = (around(1), around(NZ - 1))
     barrier = pltpu.get_barrier_semaphore()
-    for other in (*ways, (x, sibling), along(0, 1), along(0, 3), along(1, 1), along(1, 3)):
+    for other in (*ways, (x, sibling), *(along(axis, step) for axis in range(2) for step in (1, 2, 3))):
         pl.semaphore_signal(barrier, inc=1, device_id=other, device_id_type=MESH)
-    pl.semaphore_wait(barrier, 7)
+    pl.semaphore_wait(barrier, 9)
 
     def copy(src, dst, send_sem, recv_sem, other):
         return pltpu.make_async_remote_copy(
@@ -287,24 +296,25 @@
         value = hsm[at, row, shift + r]
         return value // 256, value % 256
 
+    row_of_lane = lax.broadcasted_iota(i32, (1, 128), 1) % ROWS
+
     def slots(entries, who, r):
         found = []
         for entry in entries:
-            start, grains = place_of(entry + who * (LISTS + 1), entry, r)
+            start, rows = place_of(entry + who * (LISTS + 1), entry, r)
             own = entry == LISTS
             base = 2 * CAPS[0] if own and not who else 0
-            cap = STAY if own else CAPS[entry % HOPS]
-            found.append((start, grains, base, cap))
+            found.append((start, rows, base, STAY if own else CAPS[entry % HOPS]))
         out = []
         for i in range(8):
-            start, grains, base, cap = found[0]
-            slot = base + jnp.minimum(start + i, cap - 1)
-            if len(found) == 1:
-                out.append((None, slot, None, i < grains))
-            else:
-                start_2, grains_2, _, cap_2 = found[1]
-                slot_2 = jnp.clip(start_2 + i - grains, 0, cap_2 - 1)
-                out.append((i < grains, slot, slot_2, i < grains + grains_2))
+            places = [base + jnp.minimum(start // ROWS + i, cap - 1) for start, _, base, cap in found]
+            start, rows = found[0][0:2]
+            in_first = None
+            if len(found) == 2:
+                in_first = rows > 0
+                start, rows = jnp.where(in_first, start, found[1][0]), jnp.where(in_first, rows, found[1][1])
+            at = row_of_lane + ((start // ROWS + i) * ROWS - start)
+            out.append((in_first, places[0], places[-1], (at >= 0) & (at < rows)))
         return out
 
     def sources(entries, who, mine, theirs, own):
@@ -387,8 +397,7 @@
     ]
 
     def reducer(part):
-        p_, ro_, rd_, sb_, u_, ro2_, rd2_, sb2_ = (buffers[part] for buffers in (p, ro, rd, sb, u, ro2, rd2, sb2))
-        rows = HALF // 2
+        p_, ro_, rd_, sb_, u_, rd2_ = (buffers[part] for buffers in (p, ro, rd, sb, u, rd2))
 
         def half_copy(src, dst, half, phase, k, axis, step):
             return copy(src, dst, sems.at[part, half, phase, k], recvs.at[part, half, phase, k], along(axis, step))
@@ -410,15 +419,9 @@
                 half_copy(sb_.at[half, 1], rd_.at[half, 1, hi], half, 0, 5, half, 3),
             ])
             axis = 1 - half
-            right, left, far = triple(other)
-            lo, hi = pl.ds(0, rows), pl.ds(rows, rows)
             second.append([
-                half_copy(u_.at[half, far, lo], ro2_.at[half, 0], half, 1, 0, axis, 1),
-                half_copy(u_.at[half, far, hi], ro2_.at[half, 1], half, 1, 1, axis, 3),
-                half_copy(u_.at[half, right, hi], rd2_.at[half, 0, hi], half, 1, 2, axis, 1),
-                half_copy(u_.at[half, left, lo], rd2_.at[half, 1, lo], half, 1, 3, axis, 3),
-                half_copy(sb2_.at[half, 0], rd2_.at[half, 0, lo], half, 1, 4, axis, 1),
-                half_copy(sb2_.at[half, 1], rd2_.at[half, 1, hi], half, 1, 5, axis, 3),
+                half_copy(u_.at[half, lax.rem(other + step, 4)], rd2_.at[half, step - 1], half, 1, step - 1, axis, step)
+                for step in (1, 2, 3)
             ])
 
         def begin():
@@ -456,7 +459,7 @@
                     u_[half, i] = (
                         wide_of(p_.at[half, me, i]) + wide_of(rd_.at[half, 0, i]) + wide_of(rd_.at[half, 1, i])
                     ).astype(bf16)
-                for k in range(4):
+                for k in (1, 0, 2):
                     second[half][k].start()
             if part == 0:
                 flags[1].wait_recv()
@@ -465,14 +468,7 @@
                 flags[3].start()
                 flags[4].start()
 
-        def pass_on_again():
-            for half in range(2):
-                other = x if half == 0 else y
-                for k in range(2):
-                    to = lax.rem(other + (1 if k == 0 else 3), 4)
-                    second[half][k].wait_recv()
-                    sb2_[half, k] = (wide_of(u_.at[half, to, pl.ds(k * rows, rows)]) + wide_of(ro2_.at[half, k])).astype(bf16)
-                    second[half][4 + k].start()
+        def relay():
             if part == 0:
                 flags[3].wait_recv()
                 ff[8] = ff[5] + ff[6]
@@ -481,9 +477,10 @@
         def finish():
             for half in range(2):
                 other = x if half == 0 else y
-                for k in (2, 3, 4, 5):
+                turned = wide_of(u_.at[half, other])
+                for k in range(3):
                     second[half][k].wait_recv()
-                turned = wide_of(u_.at[half, other]) + wide_of(rd2_.at[half, 0]) + wide_of(rd2_.at[half, 1])
+                    turned = turned + wide_of(rd2_.at[half, k])
                 total[half, :, part * HALF : (part + 1) * HALF] = turned.T
             if part == 0:
                 flags[4].wait_recv()
@@ -494,7 +491,7 @@
             for c in (*first[0], *first[1], *second[0], *second[1]):
                 c.wait_send()
 
-        return begin, (pass_on, turn, pass_on_again, finish), drain
+        return begin, (pass_on, turn, relay, finish), drain
 
     begin_a, steps_a, drain_a = reducer(0)
     begin_b, steps_b, drain_b = reducer(1)
@@ -570,7 +567,7 @@
 def exchange(send, send_b, send_w, head):
     vmem = pl.BlockSpec(memory_space=pltpu.VMEM)
     members = send.shape[2] - HALF
-    square, slab, thin = (members, members), (HALF, members), (HALF // 2, members)
+    square, slab = (members, members), (HALF, members)
     dma = pltpu.SemaphoreType.DMA
     panels = [pltpu.VMEM((cap, ROWS, members + HALF), bf16) for cap in CAPS] * 2
     others = [pltpu.VMEM((cap, ROWS, HALF), bf16) for cap in CAPS] * 2
@@ -607,9 +604,7 @@
             *[pltpu.VMEM((2, 2, 4, *slab), bf16)] * 2,
             *[pltpu.VMEM((2, 2, 2, *slab), bf16)] * 2,
             *[pltpu.VMEM((2, 4, *slab), bf16)] * 2,
-            *[pltpu.VMEM((2, 2, *thin), bf16)] * 2,
-            *[pltpu.VMEM((2, 2, *slab), bf16)] * 2,
-            *[pltpu.VMEM((2, 2, *thin), bf16)] * 2,
+            *[pltpu.VMEM((2, 3, *slab), bf16)] * 2,
             dma((2, HOPS, 6 + HOPS)),
             dma((2, HOPS, 6 + HOPS)),
             dma((LISTS + 1, 4)),

time: 137 us -> 130 us (0.949)
  Pallas kernels: 118 us -> 110 us
    pallas_call x1, Pallas kernels: 109 us -> 102 us  [exchange(): pl.pallas_call(exchange_kernel, out_shape=(jax.ShapeDtypeStruct((2, *squa...]
where the time goes in v4:
time: 130 us; the launch traced here: 128 us
  Pallas kernels  110 us (85%)
  between operations  14.8 us (11%)
  local copies, waits for them, and re-layouts  3.81 us (3%)
    pallas_call x1, Pallas kernels, exchange(): pl.pallas_call(exchange_kernel, out_shape=(jax.ShapeDtypeStruct((2, *squa...  102 us
    pallas_call x1, Pallas kernels, pack(): pl.pallas_call(pack_kernel, out_shape=(jax.ShapeDtypeStruct((SEND + SPARE...  4.52 us
    pallas_call x1, Pallas kernels, update(): pl.pallas_call(update_kernel, grid=(blocks, width // step), out_shape=(ja...  3.36 us
    unnamed x14, local copies, waits for them, and re-layouts  3.23 us

profile of v4, /device:TPU:8, one launch (start us, length us, event | category | flops | bytes accessed | tf_op | source)
XLA Modules:
  0.0 128.5 jit_solution(17840417131574035523)
XLA Ops:
  7.2 0.0 copy-start.2
  7.2 0.0 copy-start.3
  7.2 0.0 copy-start.4
  7.2 0.0 copy-start.5
  7.2 0.0 copy-start.6
  7.2 4.5 %shard_map.104 = (bf16[152,16,384]{2,1,0:T(8,128)(2,1)S(1)}, bf16[152,16,128]{2,1,0:T(8,128)(2,1)S(1)}, f32[152,128]{1,0:T(8,128)S(1)}, s32[8,128]{1,0:T(8,128)S(1)}) custom-call(s32[32]{0:T(128)} %bitcast.70, s32[32]{0:T(128)} %count.1, s32[6,32]{1,0:T(8,128)} %bitcast.67, s32[32,64]{1,0:T(8,128)} %pos.1, f32[32,64]{1,0:T(8,128)} %rinv.1, ...), custom_call_target="tpu_custom_call" | custom-call | tf_op jit(solution)/shard_map/pallas_call | solution.py:187
  11.7 102.0 %shard_map.105 = (f32[2,256,256]{2,1,0:T(8,128)S(1)}, f32[8,128]{1,0:T(8,128)S(1)}) custom-call(bf16[152,16,384]{2,1,0:T(8,128)(2,1)S(1)} %get-tuple-element.187.send, bf16[152,16,128]{2,1,0:T(8,128)(2,1)S(1)} %get-tuple-element.188.send_b, f32[152,128]{1,0:T(8,128)S(1)} %get-tuple-element.189.send_w, s32[8,128]{1,0:T(8,128)S(1)} %get-tuple-element.190.head), custom_call_target="tpu_custom_call" | custom-call | tf_op jit(solution)/shard_map/pallas_call | solution.py:575
  113.8 0.6 slice.19
  115.0 0.0 copy-done.2
  115.0 0.0 copy-done.3
  115.0 0.0 copy-done.4
  115.0 0.0 copy-done.5
  115.0 0.0 copy-done.6
  115.0 0.0 copy-start.1
  115.1 1.0 copy-done.1
  116.1 0.0 copy-start
  116.1 2.2 %copy-done = bf16[1,2,4096,256]{3,2,1,0:T(8,128)(2,1)S(1)} copy-done((bf16[1,2,4096,256]{3,2,1,0:T(8,128)(2,1)S(1)}, bf16[1,2,4096,256]{3,2,1,0:T(8,128)(2,1)}, u32[]{:S(2)}) %copy-start) | copy-done | bytes 4194328
  118.3 3.4 %shard_map.106 = (bf16[1,2,4096,256]{3,2,1,0:T(8,128)(2,1)}, f32[1,2,256,256]{3,2,1,0:T(8,128)}) custom-call(bf16[1,2,4096,256]{3,2,1,0:T(8,128)(2,1)S(1)} %copy-done, f32[1,2,256,256]{3,2,1,0:T(8,128)S(1)} %copy-done.1, f32[2,256,256]{2,1,0:T(8,128)S(1)} %get-tuple-element.246.total), custom_call_target="tpu_custom_call" | custom-call | tf_op jit(solution)/shard_map/pallas_call | solution.py:639
  (1 shorter events, 0.0 us)
Async XLA Ops:
  7.2 107.8 %copy-start.2 = (s32[32,64]{1,0:T(8,128)S(1)}, s32[32,64]{1,0:T(8,128)}, u32[]{:S(2)}) copy-start(s32[32,64]{1,0:T(8,128)} %pos.1) | copy-start | bytes 24580
  7.2 107.8 %copy-start.3 = (f32[32,64]{1,0:T(8,128)S(1)}, f32[32,64]{1,0:T(8,128)}, u32[]{:S(2)}) copy-start(f32[32,64]{1,0:T(8,128)} %rinv.1) | copy-start | bytes 24580
  7.2 107.8 %copy-start.4 = (s32[32,6]{0,1:T(8,128)S(1)}, s32[32,6]{0,1:T(8,128)}, u32[]{:S(2)}) copy-start(s32[32,6]{0,1:T(8,128)} %param.19) | copy-start | bytes 2308
  7.2 107.8 %copy-start.5 = (s32[32]{0:T(128)S(1)}, s32[32]{0:T(128)}, u32[]{:S(2)}) copy-start(s32[32]{0:T(128)} %count.1) | copy-start | bytes 388
  7.2 107.8 %copy-start.6 = (s32[32,1]{0,1:T(1,128)S(1)}, s32[32,1]{0,1:T(1,128)}, u32[]{:S(2)}) copy-start(s32[32,1]{0,1:T(1,128)} %param.18) | copy-start | bytes 388
  115.0 1.0 copy-start.1
  116.1 2.2 %copy-start = (bf16[1,2,4096,256]{3,2,1,0:T(8,128)(2,1)S(1)}, bf16[1,2,4096,256]{3,2,1,0:T(8,128)(2,1)}, u32[]{:S(2)}) copy-start(bf16[1,2,4096,256]{3,2,1,0:T(8,128)(2,1)} %state.1) | copy-start | bytes 12582916

commit v5 on v4

--- a/solution.py
+++ b/solution.py
@@ -510,7 +510,7 @@
             entry = way * HOPS + hop
             side[entry][1].start()
             side[entry][2].start()
-        if hop == HOPS - 2:
+        if hop == HOPS - 1:
             for k in range(HOPS):
                 for way in range(2):
                     z_copies[way][0][6 + k].start()
@@ -632,7 +632,7 @@
 
 def update(state, coeff, total):
     _, blocks, width, members = state.shape
-    step = 2048
+    step = 4096
     square = (members, members)
     rows = pl.BlockSpec((None, None, step, members), lambda j, i: (0, j, i, 0))
     one = pl.BlockSpec((None, None, *square), lambda j, i: (0, j, 0, 0))
@@ -643,7 +643,7 @@
         in_specs=[rows, one, pl.BlockSpec((None, *square), lambda j, i: (j, 0, 0))],
         out_specs=(rows, one),
         scratch_shapes=[pltpu.VMEM(square, bf16)],
-        compiler_params=pltpu.CompilerParams(vmem_limit_bytes=16 * MIB),
+        compiler_params=pltpu.CompilerParams(vmem_limit_bytes=60 * MIB),
     )(state, coeff, total)
 
 

time: 130 us -> 127 us (0.977)
  local copies, waits for them, and re-layouts: 3.81 us -> 0.61 us
    unnamed x14 -> x12, local copies, waits for them, and re-layouts: 3.23 us -> 0.03 us
where the time goes in v5:
time: 127 us; the launch traced here: 126 us
  Pallas kernels  111 us (87%)
  between operations  14.8 us (12%)
    pallas_call x1, Pallas kernels, exchange(): pl.pallas_call(exchange_kernel, out_shape=(jax.ShapeDtypeStruct((2, *squa...  102 us
    pallas_call x1, Pallas kernels, pack(): pl.pallas_call(pack_kernel, out_shape=(jax.ShapeDtypeStruct((SEND + SPARE...  4.56 us
    pallas_call x1, Pallas kernels, update(): pl.pallas_call(update_kernel, grid=(blocks, width // step), out_shape=(ja...  4.54 us

profile of v5, /device:TPU:8, one launch (start us, length us, event | category | flops | bytes accessed | tf_op | source)
XLA Modules:
  0.0 126.3 jit_solution(8267719366632311362)
XLA Ops:
  7.2 0.0 copy-start
  7.2 0.0 copy-start.1
  7.2 0.0 copy-start.2
  7.2 0.0 copy-start.3
  7.2 0.0 copy-start.4
  7.2 0.0 copy-start.5
  7.2 4.6 %shard_map.104 = (bf16[152,16,384]{2,1,0:T(8,128)(2,1)S(1)}, bf16[152,16,128]{2,1,0:T(8,128)(2,1)S(1)}, f32[152,128]{1,0:T(8,128)S(1)}, s32[8,128]{1,0:T(8,128)S(1)}) custom-call(s32[32]{0:T(128)} %bitcast.70, s32[32]{0:T(128)} %count.1, s32[6,32]{1,0:T(8,128)} %bitcast.67, s32[32,64]{1,0:T(8,128)} %pos.1, f32[32,64]{1,0:T(8,128)} %rinv.1, ...), custom_call_target="tpu_custom_call" | custom-call | tf_op jit(solution)/shard_map/pallas_call | solution.py:187
  11.8 101.8 %shard_map.105 = (f32[2,256,256]{2,1,0:T(8,128)}, f32[8,128]{1,0:T(8,128)S(1)}) custom-call(bf16[152,16,384]{2,1,0:T(8,128)(2,1)S(1)} %get-tuple-element.187.send, bf16[152,16,128]{2,1,0:T(8,128)(2,1)S(1)} %get-tuple-element.188.send_b, f32[152,128]{1,0:T(8,128)S(1)} %get-tuple-element.189.send_w, s32[8,128]{1,0:T(8,128)S(1)} %get-tuple-element.190.head), custom_call_target="tpu_custom_call" | custom-call | tf_op jit(solution)/shard_map/pallas_call | solution.py:575
  113.6 0.6 slice.19
  114.8 0.0 copy-done
  114.9 0.0 copy-done.1
  114.9 0.0 copy-done.2
  114.9 0.0 copy-done.3
  114.9 0.0 copy-done.4
  114.9 0.0 copy-done.5
  114.9 4.5 %shard_map.106 = (bf16[1,2,4096,256]{3,2,1,0:T(8,128)(2,1)}, f32[1,2,256,256]{3,2,1,0:T(8,128)}) custom-call(bf16[1,2,4096,256]{3,2,1,0:T(8,128)(2,1)} %state.1, f32[1,2,256,256]{3,2,1,0:T(8,128)} %coeff.1, f32[2,256,256]{2,1,0:T(8,128)} %get-tuple-element.246.total), custom_call_target="tpu_custom_call" | custom-call | tf_op jit(solution)/shard_map/pallas_call | solution.py:639
  (1 shorter events, 0.0 us)
Async XLA Ops:
  7.2 107.7 %copy-start = (bf16[32,64,256]{2,1,0:T(8,128)(2,1)S(1)}, bf16[32,64,256]{2,1,0:T(8,128)(2,1)}, u32[]{:S(2)}) copy-start(bf16[32,64,256]{2,1,0:T(8,128)(2,1)} %anom.1) | copy-start | bytes 3145732
  7.2 107.7 %copy-start.1 = (s32[32,64]{1,0:T(8,128)S(1)}, s32[32,64]{1,0:T(8,128)}, u32[]{:S(2)}) copy-start(s32[32,64]{1,0:T(8,128)} %pos.1) | copy-start | bytes 24580
  7.2 107.7 %copy-start.2 = (f32[32,64]{1,0:T(8,128)S(1)}, f32[32,64]{1,0:T(8,128)}, u32[]{:S(2)}) copy-start(f32[32,64]{1,0:T(8,128)} %rinv.1) | copy-start | bytes 24580
  7.2 107.7 %copy-start.3 = (s32[32,6]{0,1:T(8,128)S(1)}, s32[32,6]{0,1:T(8,128)}, u32[]{:S(2)}) copy-start(s32[32,6]{0,1:T(8,128)} %param.19) | copy-start | bytes 2308
  7.2 107.7 %copy-start.4 = (s32[32]{0:T(128)S(1)}, s32[32]{0:T(128)}, u32[]{:S(2)}) copy-start(s32[32]{0:T(128)} %count.1) | copy-start | bytes 388
  7.2 107.7 %copy-start.5 = (s32[32,1]{0,1:T(1,128)S(1)}, s32[32,1]{0,1:T(1,128)}, u32[]{:S(2)}) copy-start(s32[32,1]{0,1:T(1,128)} %param.18) | copy-start | bytes 388

commit v6 on v5

--- a/solution.py
+++ b/solution.py
@@ -534,16 +534,14 @@
                     z_copies[way][hop + 1][6 + k].start()
         for way in range(2):
             side[way * HOPS + hop][3].start()
+        steps_a[hop]()
         if hop == 0:
             side[LISTS][3].wait_recv()
             other_columns(0)
-            steps_a[0]()
         else:
             for way in range(2):
                 side[way * HOPS + hop - 1][3].wait_recv()
                 other_columns(1 + 2 * (hop - 1) + way)
-                if way == 0:
-                    steps_a[hop]()
     for entry in far_stage:
         side[entry][3].wait_recv()
     other_columns(STAGES - 1)

time: 127 us -> 128 us (level)
  no operation moved by 1% of the time
where the time goes in v6:
time: 128 us; the launch traced here: 127 us
  Pallas kernels  112 us (88%)
  between operations  14.8 us (12%)
    pallas_call x1, Pallas kernels, exchange(): pl.pallas_call(exchange_kernel, out_shape=(jax.ShapeDtypeStruct((2, *squa...  103 us
    pallas_call x1, Pallas kernels, pack(): pl.pallas_call(pack_kernel, out_shape=(jax.ShapeDtypeStruct((SEND + SPARE...  4.55 us
    pallas_call x1, Pallas kernels, update(): pl.pallas_call(update_kernel, grid=(blocks, width // step), out_shape=(ja...  4.53 us

profile of v6, /device:TPU:8, one launch (start us, length us, event | category | flops | bytes accessed | tf_op | source)
XLA Modules:
  0.0 127.4 jit_solution(17821944297904098358)
XLA Ops:
  7.2 0.0 copy-start
  7.2 0.0 copy-start.1
  7.2 0.0 copy-start.2
  7.2 0.0 copy-start.3
  7.2 0.0 copy-start.4
  7.2 0.0 copy-start.5
  7.2 4.5 %shard_map.104 = (bf16[152,16,384]{2,1,0:T(8,128)(2,1)S(1)}, bf16[152,16,128]{2,1,0:T(8,128)(2,1)S(1)}, f32[152,128]{1,0:T(8,128)S(1)}, s32[8,128]{1,0:T(8,128)S(1)}) custom-call(s32[32]{0:T(128)} %bitcast.70, s32[32]{0:T(128)} %count.1, s32[6,32]{1,0:T(8,128)} %bitcast.67, s32[32,64]{1,0:T(8,128)} %pos.1, f32[32,64]{1,0:T(8,128)} %rinv.1, ...), custom_call_target="tpu_custom_call" | custom-call | tf_op jit(solution)/shard_map/pallas_call | solution.py:187
  11.8 102.9 %shard_map.105 = (f32[2,256,256]{2,1,0:T(8,128)}, f32[8,128]{1,0:T(8,128)S(1)}) custom-call(bf16[152,16,384]{2,1,0:T(8,128)(2,1)S(1)} %get-tuple-element.187.send, bf16[152,16,128]{2,1,0:T(8,128)(2,1)S(1)} %get-tuple-element.188.send_b, f32[152,128]{1,0:T(8,128)S(1)} %get-tuple-element.189.send_w, s32[8,128]{1,0:T(8,128)S(1)} %get-tuple-element.190.head), custom_call_target="tpu_custom_call" | custom-call | tf_op jit(solution)/shard_map/pallas_call | solution.py:573
  114.7 0.6 slice.19
  115.9 0.0 copy-done
  115.9 0.0 copy-done.1
  115.9 0.0 copy-done.2
  116.0 0.0 copy-done.3
  116.0 0.0 copy-done.4
  116.0 0.0 copy-done.5
  116.0 4.5 %shard_map.106 = (bf16[1,2,4096,256]{3,2,1,0:T(8,128)(2,1)}, f32[1,2,256,256]{3,2,1,0:T(8,128)}) custom-call(bf16[1,2,4096,256]{3,2,1,0:T(8,128)(2,1)} %state.1, f32[1,2,256,256]{3,2,1,0:T(8,128)} %coeff.1, f32[2,256,256]{2,1,0:T(8,128)} %get-tuple-element.246.total), custom_call_target="tpu_custom_call" | custom-call | tf_op jit(solution)/shard_map/pallas_call | solution.py:637
  (1 shorter events, 0.0 us)
Async XLA Ops:
  7.2 108.8 %copy-start = (bf16[32,64,256]{2,1,0:T(8,128)(2,1)S(1)}, bf16[32,64,256]{2,1,0:T(8,128)(2,1)}, u32[]{:S(2)}) copy-start(bf16[32,64,256]{2,1,0:T(8,128)(2,1)} %anom.1) | copy-start | bytes 3145732
  7.2 108.8 %copy-start.1 = (s32[32,64]{1,0:T(8,128)S(1)}, s32[32,64]{1,0:T(8,128)}, u32[]{:S(2)}) copy-start(s32[32,64]{1,0:T(8,128)} %pos.1) | copy-start | bytes 24580
  7.2 108.8 %copy-start.2 = (f32[32,64]{1,0:T(8,128)S(1)}, f32[32,64]{1,0:T(8,128)}, u32[]{:S(2)}) copy-start(f32[32,64]{1,0:T(8,128)} %rinv.1) | copy-start | bytes 24580
  7.2 108.8 %copy-start.3 = (s32[32,6]{0,1:T(8,128)S(1)}, s32[32,6]{0,1:T(8,128)}, u32[]{:S(2)}) copy-start(s32[32,6]{0,1:T(8,128)} %param.19) | copy-start | bytes 2308
  7.2 108.8 %copy-start.4 = (s32[32]{0:T(128)S(1)}, s32[32]{0:T(128)}, u32[]{:S(2)}) copy-start(s32[32]{0:T(128)} %count.1) | copy-start | bytes 388
  7.2 108.8 %copy-start.5 = (s32[32,1]{0,1:T(1,128)S(1)}, s32[32,1]{0,1:T(1,128)}, u32[]{:S(2)}) copy-start(s32[32,1]{0,1:T(1,128)} %param.18) | copy-start | bytes 388
